TPU v7x, 32 devices: a whole 2x2x4 slice. The times are simulated.
32 devices in a mesh: gx: 8 (over z, y), gz: 4 (over x, core).
Axes of the slice: x: 2, y: 2, z: 4, core: 2. Of those that a mesh axis runs over, the one named last changes fastest.
Arguments:
- pressure: float32 [64, 128, 256], P('gz', 'gx'), may hold values from -6 to 6
- saturation: float32 [64, 128, 256], P('gz', 'gx'), may hold values from 0.05 to 0.8
- sat_history: float32 [64, 128, 256], P('gz', 'gx'), may hold values from 0.05 to 0.85, as said below
- storage: float32 [64, 128, 256], P('gz', 'gx'), may hold values from 0.3 to 3
- step_volume: float32 [64, 128, 256], P('gz', 'gx'), may hold values from 0.005 to 0.05
- transmiss: float32 [3, 64, 128, 256], P(None, 'gz', 'gx'), may hold values from 0.1 to 2
- perf_cell: int32 [256, 16], P('gx'), may hold values from 0 to 262143, as said below
- perf_index: float32 [256, 16], P('gx'), may hold values from 0.2 to 2
- control: int32 [256], P('gx'), may hold values from 0 to 1
- target: float32 [256], P('gx'), may hold values from 0.5 to 3
Outputs:
- new_pressure: float32 [64, 128, 256], P('gz', 'gx')
- residual: float32 [64, 128, 256], P('gz', 'gx')
- new_saturation: float32 [64, 128, 256], P('gz', 'gx')
- new_history: float32 [64, 128, 256], P('gz', 'gx')
- bottom_hole: float32 [256], P('gx')
Inputs may be any that keep to these rules, and one draw needn't show every extreme that they name: `perf_cell`: each perforation number names a cell of its own well's row of tiles, counted as layer * 16 * 256 + first lateral index within the row * 256 + second lateral index; a well's perforations lie in 16 consecutive layers, one a layer, top first, and from one to the next each lateral index moves by at most one cell. sat_history is at least the cell's saturation.
All inputs are finite; a program needn't handle non-finite values.
Results may differ from a plain program's by a relative error of at most 0.0003.
Values sent between devices are 32-bit elements; how exact they have to be, the bound alone decides.
No kernel may reach another device: no remote copies, remote signals or barrier semaphores. Data moves between devices by JAX's collectives and lax.ppermute only.
A program may use at most 64 MiB of HBM per device.

v0:
```python
import functools

import jax
import jax.numpy as jnp
from jax import lax
from jax.experimental import pallas as pl
from jax.experimental.pallas import tpu as pltpu
from jax.sharding import PartitionSpec as P

SWEEPS = 4
H = SWEEPS + 1
LANES = 128
LOADED = 4

Z_PARTS = (
    ("p0", H),
    ("tot", H),
    ("t0", H),
    ("stor", H - 1),
    ("t1", H - 1),
    ("t2", H - 1),
    ("frac", 1),
    ("sums", 1),
)


def early_parts(layers):
    own = (H, layers)
    inner = (H, layers - 1)
    return (
        ("t1", *own),
        ("tot", *own),
        ("p0", *own),
        ("dp", *own),
        ("f0", *inner),
        ("f2", *own),
        ("f1", *own),
        ("frac", *own),
        ("p0_d2", *own),
        ("f0_d2", *inner),
        ("f2_d2", *own),
        ("dp_d2", *own),
    )


def late_parts(layers):
    top = H + layers
    both = lambda name, n: ((name, H - n, n), (name, top, n))
    faces = lambda name, n: ((name, H - n, n), (name, top - 1, n))
    return (
        ("rhs", 2, layers + 6),
        ("p1_d2", 3, layers + 4),
        ("g2", 4, layers + 2),
        ("g3", H, layers),
        *both("t1", H - 1),
        *both("tot", H - 1),
        *both("p0", H - 1),
        *both("dp", H - 2),
        *faces("f0", H - 1),
        *both("f2", H - 2),
        *both("f1", H - 2),
        *both("p0_d2", H - 2),
        *faces("f0_d2", 2),
        *both("f2_d2", 1),
        *both("dp_d2", 1),
    )


def tiles(parts):
    return -(-sum(count for _, _, count in parts) // 8)


SEAMS = ("f0", "f1", "f2", "tot", "dp", "p0", "frac", "p1", "rhs2", "rhs3")
PLACES = {
    "t1": ("f1", None, 7),
    "f1": ("f1", 0, 6),
    "tot": ("tot", 0, 7),
    "p0": ("p0", 0, 7),
    "dp": ("dp", 0, 7),
    "dp_d2": ("dp", 1, 6),
    "f0": ("f0", 0, 7),
    "f0_d2": ("f0", 1, 6),
    "f2": ("f2", 0, 7),
    "f2_d2": ("f2", 1, 6),
    "frac": ("frac", 0, 7),
    "p0_d2": ("p0", 1, 6),
    "p1_d2": ("p1", 1, 6),
    "rhs": ("rhs2", 0, 7),
    "g2": ("rhs2", 1, 6),
    "g3": ("rhs3", 1, 6),
}


def pack(message, parts, refs, rows):
    at = 0
    for name, first, count in parts:
        for e in range(first, first + count):
            message[at // 8, at % 8 : at % 8 + 1, :] = refs[name][e, rows[name] : rows[name] + 1, :]
            at += 1


def pack_both(near, cross, parts, up, down, rows, gx):
    last = rows - 1
    outer = {name: 0 if PLACES[name][2] == 7 else 1 for name in PLACES}
    up_rows = {name: last - outer[name] for name in PLACES} | {"f1": last - 1}
    down_rows = dict(outer) | {"f1": 0}
    even = lax.axis_index(gx) % 2 == 0

    @pl.when(even)
    def _():
        pack(near, parts, up, up_rows)
        pack(cross, parts, down, down_rows)

    @pl.when(jnp.logical_not(even))
    def _():
        pack(cross, parts, up, up_rows)
        pack(near, parts, down, down_rows)


def unpack(message, parts, seams, side):
    at = 0
    for name, first, count in parts:
        seam, *places = PLACES[name]
        place = places[side]
        for e in range(first, first + count):
            if place is not None:
                seams[seam][e, place : place + 1, :] = message[at // 8, at % 8 : at % 8 + 1, :]
            at += 1


def unpack_both(near, cross, parts, seams, gx):
    even = lax.axis_index(gx) % 2 == 0

    @pl.when(even)
    def _():
        unpack(near, parts, seams, 0)
        unpack(cross, parts, seams, 1)

    @pl.when(jnp.logical_not(even))
    def _():
        unpack(cross, parts, seams, 0)
        unpack(near, parts, seams, 1)


def mobility(sat, history):
    trapped = history / (1.0 + 1.5 * history)
    excess = jnp.maximum(sat - trapped, 0.0)
    free_gas = 0.5 * (excess + jnp.sqrt(excess * excess + excess / 0.375))
    relperm = jnp.where(sat < history, free_gas * free_gas, sat * sat)
    gas = relperm / 0.5
    total = (1.0 - sat) * (1.0 - sat) + gas
    return (total, gas / total)


def roll(x, shift, axis):
    return pltpu.roll(x, shift % x.shape[axis], axis)


def loop(first, last, step, carry):
    count = last - first
    unroll = -(-count // -(-count // 10))
    groups = count // unroll

    def group(g, carry):
        for i in range(unroll):
            carry = step(first + g * unroll + i, carry)
        return carry

    carry = lax.fori_loop(0, groups, group, carry) if groups > 1 else group(0, carry)
    for index in range(first + groups * unroll, last):
        carry = step(index, carry)
    return carry


def split(x):
    high = x.astype(jnp.bfloat16)
    return (high, (x - high.astype(jnp.float32)).astype(jnp.bfloat16))


def at_places(cell, first_layer, layers, rows, columns):
    layer = cell // (rows * columns)
    row = (cell - layer * (rows * columns)) // columns
    place = (layer - first_layer) * rows + row
    return lax.broadcasted_iota(jnp.int32, (layers * rows, cell.shape[1]), 0) == place


def at_columns(cell, columns):
    return lax.broadcasted_iota(jnp.int32, (columns, cell.shape[1]), 0) == cell % columns


def gather(field, at_place, at_column):
    high, low = split(field)
    hot = at_column.astype(jnp.bfloat16)
    by_column = jnp.dot(high, hot, preferred_element_type=jnp.float32) + jnp.dot(
        low, hot, preferred_element_type=jnp.float32
    )
    return jnp.sum(jnp.where(at_place, by_column, 0.0), axis=0, keepdims=True)


def flatten(block, spread):
    perfs, wells = block.shape
    spread[...] = jnp.zeros(spread.shape, jnp.float32)
    spread[:, 0:wells] = block
    wide = spread[...]
    shift = wells
    while shift < LANES:
        wide = wide + roll(wide, shift, 1)
        shift *= 2
    each = LANES // wells
    entry = lax.broadcasted_iota(jnp.int32, (perfs, LANES), 0)
    group = lax.broadcasted_iota(jnp.int32, (perfs, LANES), 1) // wells
    tiles = [
        jnp.sum(jnp.where(entry == first + group, wide, 0.0), axis=0, keepdims=True)
        for first in range(0, perfs, each)
    ]
    return jnp.concatenate(tiles, axis=1)


def prepare_kernel(
    sat,
    hist,
    pressure,
    storage,
    trans,
    cell_in,
    index_in,
    control_in,
    target_in,
    p0e,
    tote,
    frace,
    stor,
    t0,
    t1,
    t2,
    near,
    cross,
    sums,
    cell,
    wells,
    perfs,
    hot,
    sat_v,
    hist_v,
    cell_v,
    index_v,
    control_v,
    target_v,
    spread,
    sems,
    *,
    gz,
):
    layers, rows, columns = pressure.shape
    ext = layers + 2 * H
    own = pl.ds(H, layers)
    parts = [(l, min(LOADED, layers - l)) for l in range(0, layers, LOADED)]
    in_parts = [
        (source.at[pl.ds(l, n)], target.at[pl.ds(offset + l, n)])
        for source, target, offset in ((sat, sat_v, 0), (hist, hist_v, 0), (pressure, p0e, H))
        for l, n in parts
    ]
    small = [(cell_in, cell_v), (index_in, index_v), (control_in, control_v), (target_in, target_v)]
    large = [
        (trans.at[0], t0.at[own]),
        (storage, stor.at[own]),
        (trans.at[1], t1.at[own]),
        (trans.at[2], t2.at[own]),
    ]
    copies = [
        pltpu.make_async_copy(a, b, sems.at[i])
        for i, (a, b) in enumerate(in_parts + small + large)
    ]
    for copy in copies:
        copy.start()

    def layer_step(l, carry):
        t, f = mobility(sat_v[l], hist_v[l])
        tote[l + H] = t
        frace[l + H] = f
        return carry

    for i, (l, n) in enumerate(parts):
        copies[i].wait()
        copies[len(parts) + i].wait()
        loop(l, l + n, layer_step, 0)
    for copy in copies[2 * len(parts) : -len(large)]:
        copy.wait()
    count, group = cell_v.shape
    cell[...] = flatten(cell_v[...].astype(jnp.float32), spread).astype(jnp.int32)
    wells[0:1, :] = flatten(index_v[...], spread)
    wells[1:2, :] = flatten(jnp.broadcast_to(target_v[...], (count, group)), spread)
    wells[2:3, :] = flatten(
        jnp.broadcast_to(control_v[...].astype(jnp.float32), (count, group)), spread
    )
    at_place = at_places(cell[...], lax.axis_index(gz) * layers, layers, rows, columns)
    at_column = at_columns(cell[...], columns)
    hot[...] = at_place.astype(jnp.bfloat16)
    flat = (layers * rows, columns)
    weight = wells[0:1, :] * gather(tote[own].reshape(flat), at_place, at_column)
    cell_p = gather(p0e[own].reshape(flat), at_place, at_column)
    perfs[0:1, :] = weight
    perfs[1:2, :] = cell_p
    for i, value in enumerate((weight * cell_p, weight)):
        part = value[:, 0:LANES]
        for lane in range(LANES, value.shape[1], LANES):
            part = part + value[:, lane : lane + LANES]
        shift = LANES // 2
        while shift >= group:
            part = part + roll(part, shift, 1)
            shift //= 2
        sums[i : i + 1, :] = part
    for copy in copies[-len(large) :]:
        copy.wait()
    even = lax.axis_index(gz) % 2 == 0
    refs = {"p0": p0e, "tot": tote, "t0": t0, "stor": stor, "t1": t1, "t2": t2, "frac": frace}
    for message, is_top in ((near, even), (cross, jnp.logical_not(even))):
        at = 0
        for name, count in Z_PARTS:
            if name == "sums" and message is cross:
                continue
            if name == "sums":
                message[at] = jnp.zeros((rows, columns), jnp.float32)
                message[at, 0:2, 0:LANES] = sums[...]
            else:
                edge = jnp.where(is_top, H + layers - count, H)
                message[pl.ds(at, count)] = refs[name][pl.ds(edge, count)]
            at += count


def masks(rows, columns):
    row = lax.broadcasted_iota(jnp.int32, (rows, columns), 0)
    column = lax.broadcasted_iota(jnp.int32, (rows, columns), 1)
    return (row == rows - 1, column == columns - 1)


def lateral_faces(tot, t1, t2, store, last_row, last_column, top_x):
    along = jnp.where(last_row, 0.0, t1) * 0.5 * (tot + roll(tot, -1, 0))
    across = jnp.where(last_column, 0.0, t2) * 0.5 * (tot + roll(tot, -1, 1))
    part = store + along + roll(along, 1, 0) + across + roll(across, 1, 1)
    return (jnp.where(last_row, jnp.where(top_x, 0.0, t1), along), across, part)


def is_last(axis):
    return lax.axis_index(axis) == lax.axis_size(axis) - 1


def first_sweep(e, p0e, stor, f0e, f1e, f2e, dpe, last_row):
    above = f0e[e]
    below = f0e[e - 1]
    along = jnp.where(last_row, 0.0, f1e[e])
    across = f2e[e]
    diag = dpe[e] + above + below
    p = p0e[e]
    base = stor[e] * p + above * p0e[e + 1] + below * p0e[e - 1]
    base = base + along * roll(p, -1, 0) + roll(along * p, 1, 0)
    base = base + across * roll(p, -1, 1) + roll(across * p, 1, 1)
    return (base, jnp.where(diag > 0.0, 1.0 / diag, 0.0))


def faces_kernel(*refs, layers, gx):
    p0e, tote, frace, stor, t0, t1, t2, part = refs[:8]
    f0e, f1e, f2e, dpe, base, inverse, near, cross, sums = refs[8:]
    _, rows, columns = p0e.shape
    last_row, last_column = masks(rows, columns)
    top_x = is_last(gx)

    def step(e, carry):
        tot = tote[e]
        f0e[e] = t0[e] * 0.5 * (tot + tote[e + 1])
        f1e[e], f2e[e], dpe[e] = lateral_faces(
            tot, t1[e], t2[e], stor[e], last_row, last_column, top_x
        )
        return carry

    loop(H, H + layers, step, 0)
    sums[...] = part[...]
    refs = {"t1": f1e, "tot": tote, "p0": p0e, "dp": dpe, "f0": f0e, "f2": f2e, "f1": f1e}
    refs |= {"frac": frace, "p0_d2": p0e, "f0_d2": f0e, "f2_d2": f2e, "dp_d2": dpe}
    pack_both(near, cross, early_parts(layers), refs, refs, rows, gx)

    def sweep_step(e, carry):
        base[e], inverse[e] = first_sweep(e, p0e, stor, f0e, f1e, f2e, dpe, last_row)
        return carry

    loop(H + 1, H + layers - 1, sweep_step, 0)


def well_holes(sums, wells):
    repeat = lambda x: jnp.concatenate([x] * (wells.shape[1] // LANES), axis=1)
    goal = wells[1:2, :]
    return jnp.where(
        wells[2:3, :] == 0.0, (goal + repeat(sums[0:1, :])) / repeat(sums[1:2, :]), goal
    )


def join(a, b):
    return jnp.concatenate([a, b], axis=0)


def seam_faces(first, last, fields, seams, f1, inverse, p):
    p0e, tote, f0e, f1e, dpe = fields
    rows, columns = p0e.shape[1:]
    row = lax.broadcasted_iota(jnp.int32, (rows + 8, columns), 0)
    edge = (row == rows - 1) | (row == rows + 7)

    def step(e, below):
        tot = join(tote[e], seams["tot"][e])
        mixed = join(f1e[e], seams["f1"][e])
        border = jnp.where(edge, mixed * 0.5 * (tot + roll(tot, -1, 0)), 0.0)
        f1[e] = jnp.where(edge, border, mixed)
        above = join(f0e[e], seams["f0"][e])
        diag = join(dpe[e], seams["dp"][e]) + above + below + border + roll(border, 1, 0)
        inverse[e] = jnp.where(diag > 0.0, 1.0 / diag, 0.0)
        p[e] = join(p0e[e], seams["p0"][e])
        return above

    loop(first, last, step, join(f0e[first - 1], seams["f0"][first - 1]))


def sweep_layers(number, first, last, old, new, fields, seams, f1, inverse, part):
    rhse, f0e, f2e = fields
    rows, columns = rhse.shape[1:]
    row = lax.broadcasted_iota(jnp.int32, (rows + 8, columns), 0)
    beyond = (row == rows + 1) | (row == rows + 6)
    blank = jnp.zeros((rows, columns), jnp.float32)

    def step(e, carry):
        below, p = carry
        above = old[e + 1]
        face = join(f0e[e], seams["f0"][e])
        x = f1[e]
        y = join(f2e[e], seams["f2"][e])
        side = seams["rhs2"][e]
        if number == 3:
            side = jnp.where(beyond[rows:], seams["rhs3"][e], side)
        total = join(rhse[e], side) + below + face * above
        total = total + x * roll(p, -1, 0) + roll(x * p, 1, 0)
        total = total + y * roll(p, -1, 1) + roll(y * p, 1, 1)
        value = total * inverse[e]
        if number == 1:
            value = jnp.where(beyond, join(blank, seams["p1"][e]), value)
        new[e, part] = value[part]
        return (face * p, above)

    start = join(f0e[first - 1], seams["f0"][first - 1]) * old[first - 1]
    loop(first, last, step, (start, old[first]))


def seam_kernel(near, cross, *refs, layers, gx):
    p0e, tote, f0e, f1e, f2e, dpe, rhse = refs[:7]
    refs = refs[7:]
    seams = dict(zip(SEAMS, refs))
    f1, inverse, p, p1 = refs[len(SEAMS) :]
    for seam in seams.values():
        seam[...] = jnp.zeros(seam.shape, jnp.float32)
    unpack_both(near, cross, early_parts(layers), seams, gx)
    inner = (H + 1, H + layers - 1)
    seam_faces(*inner, (p0e, tote, f0e, f1e, dpe), seams, f1, inverse, p)
    for e in (H, H + layers - 1):
        p[e] = join(p0e[e], jnp.zeros_like(seams["p0"][e]))
    own = slice(0, p0e.shape[1])
    sweep_layers(1, *inner, p, p1, (rhse, f0e, f2e), seams, f1, inverse, own)


def halo_kernel(*refs, layers, gx, gz):
    own_t0, cross, near, cell, wells, own_perfs = refs[10:16]
    p0e, tote, frace, stor, f0e, f1e, f2e, dpe, base, inverse, perfs, hot = refs[16:]
    ext, rows, columns = p0e.shape
    even = lax.axis_index(gz) % 2 == 0
    top_z = is_last(gz)
    top_x = is_last(gx)
    last_row, last_column = masks(rows, columns)
    where = {}
    at = 0
    for name, count in Z_PARTS:
        where[name] = (at, count)
        at += count

    def halo(name, e):
        at, count = where[name]
        low = e < H
        at = at + e - (H - count if low else H + layers)
        one, two = (near[at], cross[at])
        return jnp.where(even, two, one) if low else jnp.where(even, one, two)

    for name, target in (("p0", p0e), ("tot", tote), ("frac", frace), ("stor", stor)):
        count = where[name][1]
        for e in (*range(H - count, H), *range(H + layers, H + layers + count)):
            target[e] = halo(name, e)
    f0e[H + layers - 1] = jnp.where(top_z, 0.0, own_t0[H + layers - 1]) * 0.5 * (
        tote[H + layers - 1] + tote[H + layers]
    )
    for e in (*range(0, H), *range(H + layers, ext - 1)):
        f0e[e] = halo("t0", e) * 0.5 * (tote[e] + tote[e + 1])
    for e in (*range(1, H), *range(H + layers, ext - 1)):
        f1e[e], f2e[e], dpe[e] = lateral_faces(
            tote[e], halo("t1", e), halo("t2", e), stor[e], last_row, last_column, top_x
        )
    for e in (*range(1, H + 1), *range(H + layers - 1, ext - 1)):
        base[e], inverse[e] = first_sweep(e, p0e, stor, f0e, f1e, f2e, dpe, last_row)
    width = H - 1
    first = lax.axis_index(gz) * layers
    sides = ((1, first - width), (H + layers, first + layers))
    at_place = [at_places(cell[...], layer, width, rows, columns) for _, layer in sides]
    at_place = jnp.concatenate(at_place, axis=0)
    at_column = at_columns(cell[...], columns)
    hot[...] = at_place.astype(jnp.bfloat16)
    flat = (width * rows, columns)
    both = lambda ref: join(*(ref[e : e + width].reshape(flat) for e, _ in sides))
    weight = wells[0:1, :] * gather(both(tote), at_place, at_column)
    perfs[0:1, :] = own_perfs[0:1, :] + weight
    perfs[1:2, :] = own_perfs[1:2, :] + gather(both(p0e), at_place, at_column)


def build_kernel(*refs, layers, gx):
    p0e, stor, f0e, f1e, f2e, dpe, tote, base, inverse, sums, perfs, hot, own_hot = refs[:13]
    cell, wells, rhse, source, x_near, x_cross, bottom, p1, g2u, g2d, g3u, g3d = refs[13:]
    ext, rows, columns = p0e.shape
    last_row, _ = masks(rows, columns)
    hole = well_holes(sums[...], wells[...])
    bottom[...] = hole[:, 0:LANES]
    rate = perfs[0:1, :] * (hole - perfs[1:2, :])
    pieces = split(jnp.where(at_columns(cell[...], columns), rate, 0.0))

    def scatter(mask):
        spread = [
            lax.dot_general(
                mask, piece, (((1,), (1,)), ((), ())), preferred_element_type=jnp.float32
            )
            for piece in pieces
        ]
        return (spread[0] + spread[1]).reshape(-1, rows, columns)

    width = H - 1
    inside = scatter(own_hot[...])
    outside = scatter(hot[...])
    source[...] = inside
    rhse[H : ext - H] = inside
    rhse[1:H] = outside[:width]
    rhse[ext - H : ext - 1] = outside[width:]

    def first_step(e, carry):
        wells_rate = rhse[e]
        p1[e] = (base[e] + wells_rate) * inverse[e]
        rhse[e] = stor[e] * p0e[e] + wells_rate
        return carry

    loop(1, ext - 1, first_step, 0)

    def second_step(e, carry):
        along = jnp.where(last_row, 0.0, f1e[e])
        across = f2e[e]
        p = p1[e]
        rhs = rhse[e]
        lower = roll(along * p, 1, 0)
        upper = along * roll(p, -1, 0)
        g2u[e] = rhs + lower
        g2d[e] = rhs + upper
        new = rhs + lower + upper + f0e[e] * p1[e + 1] + f0e[e - 1] * p1[e - 1]
        new = new + across * roll(p, -1, 1) + roll(across * p, 1, 1)
        p2 = new * inverse[e]
        g3u[e] = rhs + roll(along * p2, 1, 0)
        g3d[e] = rhs + along * roll(p2, -1, 0)
        return carry

    loop(H - 1, ext - H + 1, second_step, 0)

    shared = {"t1": f1e, "tot": tote, "p0": p0e, "dp": dpe, "f0": f0e, "f2": f2e, "f1": f1e}
    shared |= {"p0_d2": p0e, "f0_d2": f0e, "f2_d2": f2e, "dp_d2": dpe, "rhs": rhse, "p1_d2": p1}
    up = shared | {"g2": g2u, "g3": g3u}
    down = shared | {"g2": g2d, "g3": g3d}
    pack_both(x_near, x_cross, late_parts(layers), up, down, rows, gx)


def finish_kernel(*refs, gx):
    sat, hist, volume, storage, source = refs[:5]
    p0e, tote, frace, f0e, f1e, f2e, dpe, rhse, near, cross = refs[5:15]
    hole = refs[19 + len(SEAMS)]
    refs = refs[20 + len(SEAMS) :]
    new_p, residual, new_sat, new_hist, bottom = refs[:5]
    seams = dict(zip(SEAMS, refs[5:]))
    f1, rdiag, pa, pb = refs[5 + len(SEAMS) :]
    bottom[...] = hole[:, 0 : bottom.shape[1]]
    layers, rows, columns = sat.shape
    ext = layers + 2 * H
    unpack_both(near, cross, late_parts(layers), seams, gx)
    sfrac = seams["frac"]
    pa[0] = join(p0e[0], seams["p0"][0])
    pa[ext - 1] = join(p0e[ext - 1], seams["p0"][ext - 1])
    for first, last in ((1, H + 1), (ext - H - 1, ext - 1)):
        seam_faces(first, last, (p0e, tote, f0e, f1e, dpe), seams, f1, rdiag, pa)

    pressures = (pa, pb)
    fields = (rhse, f0e, f2e)
    inner = (H + 1, ext - H - 1)
    everywhere = slice(0, rows + 8)
    for number in range(1, SWEEPS + 1):
        old, new = pressures[(number - 1) % 2], pressures[number % 2]
        ranges = [(number, ext - number, everywhere)]
        if number == 1:
            ranges = [
                (number, inner[0], everywhere),
                (*inner, slice(rows, rows + 8)),
                (inner[1], ext - number, everywhere),
            ]
        for first, last, part in ranges:
            sweep_layers(number, first, last, old, new, fields, seams, f1, rdiag, part)
    field = pressures[SWEEPS % 2]

    def flow(face, p, p_next, f, f_next):
        water = face * (p - p_next)
        return (water, water * jnp.where(water > 0, f, f_next))

    def last_step(l, carry):
        below_w, below_g = carry
        e = l + H
        p = field[e]
        f = join(frace[e], sfrac[e])
        own_p = p[:rows]
        own_f = f[:rows]
        above_w, above_g = flow(f0e[e], own_p, field[e + 1][:rows], own_f, frace[e + 1])
        xw, xg = flow(f1[e], p, roll(p, -1, 0), f, roll(f, -1, 0))
        yw, yg = flow(f2e[e], own_p, roll(own_p, -1, 1), own_f, roll(own_f, -1, 1))
        water = above_w - below_w + (xw - roll(xw, 1, 0))[:rows] + yw - roll(yw, 1, 1)
        out = above_g - below_g + (xg - roll(xg, 1, 0))[:rows] + yg - roll(yg, 1, 1)
        new_p[l] = own_p
        residual[l] = rhse[e] - storage[l] * own_p - water
        src = source[l]
        gas = jnp.maximum(src, 0.0) + jnp.minimum(src, 0.0) * own_f
        s = sat[l] + volume[l] * (gas - out)
        new_sat[l] = s
        new_hist[l] = jnp.maximum(hist[l], s)
        return (above_w, above_g)

    first = flow(f0e[H - 1], field[H - 1][:rows], field[H][:rows], frace[H - 1], frace[H])
    loop(0, layers, last_step, first)


def swap(block, axis, first):
    pairs = [(i, i + 1) for i in range(first, lax.axis_size(axis) - 1, 2)]
    return lax.ppermute(block, axis, pairs + [(b, a) for a, b in pairs])


def pin(*shape, dtype=jnp.float32):
    return pltpu.VMEM(shape, dtype)


VMEM = pl.BlockSpec(memory_space=pltpu.VMEM)
HBM = pl.BlockSpec(memory_space=pltpu.HBM)


def call(kernel, outs, scratch, *args, space=VMEM, sems=0, aliases={}):
    as_struct = lambda s: s if hasattr(s, "dtype") else jax.ShapeDtypeStruct(s, jnp.float32)
    as_scratch = lambda s: pltpu.VMEM(as_struct(s).shape, as_struct(s).dtype)
    return pl.pallas_call(
        kernel,
        out_shape=[as_struct(s) for s in outs],
        in_specs=[space] * len(args),
        out_specs=[VMEM] * len(outs),
        scratch_shapes=[as_scratch(s) for s in scratch]
        + ([pltpu.SemaphoreType.DMA((sems,))] if sems else []),
        input_output_aliases=aliases,
        compiler_params=pltpu.CompilerParams(vmem_limit_bytes=24 * 1024 * 1024),
    )(*(pltpu.with_memory_space_constraint(a, pltpu.HBM) if space is HBM else a for a in args))


def body(
    pressure,
    saturation,
    sat_history,
    storage,
    step_volume,
    transmiss,
    perf_cell,
    perf_index,
    control,
    target,
):
    layers, rows, columns = pressure.shape
    ext = layers + 2 * H
    wells, perfs = perf_cell.shape
    block = (layers, rows, columns)
    pinned = pin(*block)
    ext_block = pin(ext, rows, columns)
    z_layers = sum(count for _, count in Z_PARTS)
    z_near, z_cross = (pin(n, rows, columns) for n in (z_layers, z_layers - 1))
    entries = wells * perfs
    early, late = (pin(tiles(f(layers)), 8, columns) for f in (early_parts, late_parts))
    seams = [pin(ext, 8, columns)] * len(SEAMS)
    *fields, near, cross, part, cell, per_perf, perf_values, own_hot = call(
        functools.partial(prepare_kernel, gz="gz"),
        [ext_block] * 7
        + [z_near, z_cross]
        + [
            pin(2, LANES),
            pin(1, entries, dtype=jnp.int32),
            pin(3, entries),
            pin(2, entries),
            pin(layers * rows, entries, dtype=jnp.bfloat16),
        ],
        [
            block,
            block,
            jax.ShapeDtypeStruct((perfs, wells), jnp.int32),
            (perfs, wells),
            jax.ShapeDtypeStruct((1, wells), jnp.int32),
            (1, wells),
            (perfs, LANES),
        ],
        saturation,
        sat_history,
        pressure,
        storage,
        transmiss,
        perf_cell.T,
        perf_index.T,
        control.reshape(1, wells),
        target.reshape(1, wells),
        space=HBM,
        sems=3 * -(-layers // LOADED) + 8,
    )
    cross = swap(cross, "gz", 1)
    near = swap(near, "gz", 0)
    p0e, tote, frace, stor, t0, t1, t2 = fields
    f0e, f1e, f2e, dpe, base, inverse, early_near, early_cross, part = call(
        functools.partial(faces_kernel, layers=layers, gx="gx"),
        [ext_block] * 6 + [early, early, pin(2, LANES)],
        [],
        *fields,
        part,
    )
    early_cross = swap(early_cross, "gx", 1)
    early_near = swap(early_near, "gx", 0)
    sums = part + near[-1, 0:2, 0:LANES]
    step = 2
    while step < lax.axis_size("gz"):
        pairs = [(i, i ^ step) for i in range(lax.axis_size("gz"))]
        tile = jnp.pad(sums, ((0, 8 - sums.shape[0]), (0, 0)))
        sums = sums + lax.ppermute(tile, "gz", pairs)[: sums.shape[0]]
        step *= 2
    p0e, tote, frace, stor, f0e, f1e, f2e, dpe, base, inverse, perf_values, hot = call(
        functools.partial(halo_kernel, layers=layers, gx="gx", gz="gz"),
        [ext_block] * 10
        + [pin(2, entries), pin(2 * (H - 1) * rows, entries, dtype=jnp.bfloat16)],
        [],
        p0e,
        tote,
        frace,
        stor,
        f0e,
        f1e,
        f2e,
        dpe,
        base,
        inverse,
        t0,
        cross,
        near,
        cell,
        per_perf,
        perf_values,
        aliases={i: i for i in range(10)},
    )
    rhse, source, late_near, late_cross, hole = call(
        functools.partial(build_kernel, layers=layers, gx="gx"),
        [ext_block, pinned, late, late, pin(1, LANES)],
        [ext_block] * 5,
        p0e,
        stor,
        f0e,
        f1e,
        f2e,
        dpe,
        tote,
        base,
        inverse,
        sums,
        perf_values,
        hot,
        own_hot,
        cell,
        per_perf,
    )
    late_cross = swap(late_cross, "gx", 1)
    late_near = swap(late_near, "gx", 0)
    early_near, early_cross, rhse = lax.optimization_barrier((early_near, early_cross, rhse))
    joined = [pin(ext, rows + 8, columns)] * 4
    filled = call(
        functools.partial(seam_kernel, layers=layers, gx="gx"),
        seams + joined,
        [],
        early_near,
        early_cross,
        p0e,
        tote,
        f0e,
        f1e,
        f2e,
        dpe,
        rhse,
    )
    field, residual, new_sat, new_hist, bottom, *_ = call(
        functools.partial(finish_kernel, gx="gx"),
        [block] * 4 + [(1, wells)] + seams + joined,
        [],
        saturation,
        sat_history,
        step_volume,
        storage,
        source,
        p0e,
        tote,
        frace,
        f0e,
        f1e,
        f2e,
        dpe,
        rhse,
        late_near,
        late_cross,
        *filled,
        hole,
        aliases={15 + i: 5 + i for i in range(len(filled))},
    )
    return (field, residual, new_sat, new_hist, bottom.reshape(wells))


def solution(mesh):
    return jax.shard_map(
        body,
        mesh=mesh,
        in_specs=(
            P("gz", "gx", None),
            P("gz", "gx", None),
            P("gz", "gx", None),
            P("gz", "gx", None),
            P("gz", "gx", None),
            P(None, "gz", "gx", None),
            P("gx", None),
            P("gx", None),
            P("gx"),
            P("gx"),
        ),
        out_specs=(
            P("gz", "gx", None),
            P("gz", "gx", None),
            P("gz", "gx", None),
            P("gz", "gx", None),
            P("gx"),
        ),
        check_vma=False,
    )
```

profile of v0, /device:TPU:24, one launch (start us, length us, event | category | flops | bytes accessed | tf_op | source)
XLA Modules:
  0.0 29.4 jit_solution(2485123002439040918)
XLA Ops:
  0.6 2.4 %shard_map.137 = (f32[26,16,256]{2,1,0:T(8,128)S(1)}, f32[26,16,256]{2,1,0:T(8,128)S(1)}, f32[26,16,256]{2,1,0:T(8,128)S(1)}, f32[26,16,256]{2,1,0:T(8,128)S(1)}...) custom-call(f32[16,16,256]{2,1,0:T(8,128)} %refs_0_.1, ...), custom_call_target="tpu_custom_call" | custom-call | tf_op jit(solution)/shard_map/pallas_call | solution.py:656
  3.1 0.1 collective-permute-start.1
  3.1 0.7 %collective-permute-start = (f32[28,16,256]{2,1,0:T(8,128)S(1)}, f32[28,16,256]{2,1,0:T(8,128)S(1)}, u32[]{:S(2)}, u32[]{:S(2)}) collective-permute-start(f32[28,16,256]{2,1,0:T(8,128)S(1)} %get-tuple-element.81), channel_id=1, source_target_pairs={{1,2},{2,1},{5,6},{6,5},{9,10},{10,9},{13,14},{14,13},{17,18},{18,... | collective-permute-start | bytes 1376264 | tf_op jit(solution)/shard_map/ppermute | solution.py:642
  3.8 0.9 %shard_map.138 = (f32[26,16,256]{2,1,0:T(8,128)S(1)}, f32[26,16,256]{2,1,0:T(8,128)S(1)}, f32[26,16,256]{2,1,0:T(8,128)S(1)}, f32[26,16,256]{2,1,0:T(8,128)S(1)}...) custom-call(f32[26,16,256]{2,1,0:T(8,128)S(1)} %get-tuple-element.67, ...), custom_call_target="tpu_custom_call" | custom-call | tf_op jit(solution)/shard_map/pallas_call | solution.py:656
  4.7 0.3 collective-permute-done.1.refs_12_
  5.0 3.2 %collective-permute-start.2 = (f32[8,128]{1,0:T(8,128)S(1)}, f32[8,128]{1,0:T(8,128)S(1)}, u32[]{:S(2)}, u32[]{:S(2)}) collective-permute-start(f32[8,128]{1,0:T(8,128)S(1)} %pad.4), channel_id=1, source_target_pairs={{0,2},{1,3},{2,0},{3,1},{4,6},{5,7},{6,4},{7,5},{8,10},{9,11},{10,... | collective-permute-start | bytes 12296 | tf_op jit(solution)/shard_map/ppermute | solution.py:740
  8.1 1.5 %collective-permute-start.3 = (f32[24,8,256]{2,1,0:T(8,128)S(1)}, f32[24,8,256]{2,1,0:T(8,128)S(1)}, u32[]{:S(2)}, u32[]{:S(2)}) collective-permute-start(f32[24,8,256]{2,1,0:T(8,128)S(1)} %get-tuple-element.101), channel_id=1, source_target_pairs={{0,4},{8,12},{16,20},{24,28},{4,0},{12,8},{20,16},{28,24},{1,5},{9... | collective-permute-start | bytes 589832 | tf_op jit(solution)/shard_map/ppermute | solution.py:642
  9.7 2.3 %collective-permute-start.4 = (f32[24,8,256]{2,1,0:T(8,128)S(1)}, f32[24,8,256]{2,1,0:T(8,128)S(1)}, u32[]{:S(2)}, u32[]{:S(2)}) collective-permute-start(f32[24,8,256]{2,1,0:T(8,128)S(1)} %get-tuple-element.102), channel_id=1, source_target_pairs={{4,8},{12,16},{20,24},{8,4},{16,12},{24,20},{5,9},{13,17},{21,25},... | collective-permute-start | bytes 589832 | tf_op jit(solution)/shard_map/ppermute | solution.py:642
  12.0 0.0 collective-permute-done.refs_11_
  12.0 0.6 %shard_map.139 = (f32[26,16,256]{2,1,0:T(8,128)S(1)}, f32[26,16,256]{2,1,0:T(8,128)S(1)}, f32[26,16,256]{2,1,0:T(8,128)S(1)}, f32[26,16,256]{2,1,0:T(8,128)S(1)}...) custom-call(f32[26,16,256]{2,1,0:T(8,128)S(1)} %get-tuple-element.67, ...), custom_call_target="tpu_custom_call", output_to_operand_aliasing={{0}: (0, {}), {1}: (1, {}), {2}: (2, {}), {3}: (3, {}), {4}... | custom-call | tf_op jit(solution)/shard_map/pallas_call | solution.py:656
  12.6 1.1 %collective-permute-done.2 = f32[8,128]{1,0:T(8,128)S(1)} collective-permute-done((f32[8,128]{1,0:T(8,128)S(1)}, f32[8,128]{1,0:T(8,128)S(1)}, u32[]{:S(2)}, u32[]{:S(2)}) %collective-permute-start.2) | collective-permute-done | bytes 4128 | tf_op jit(solution)/shard_map/ppermute | solution.py:740
  13.7 1.2 %shard_map.140 = (f32[26,16,256]{2,1,0:T(8,128)S(1)}, f32[16,16,256]{2,1,0:T(8,128)S(1)}, f32[18,8,256]{2,1,0:T(8,128)S(1)}, f32[18,8,256]{2,1,0:T(8,128)S(1)}, f32[1,128]{1,0:T(1,128)S(1)}) custom-call(f32[26,16,256]{2,1,0:T(8,128)S(1)} %get-tuple-element.86.refs_0_.refs_5_, f32[26,16,256]{2,1,0:T(8,128)S(1)} %get-tuple-element.87.refs_1_, ...), custom_call_target="tpu_custom_call" | custom-call | tf_op jit(solution)/shard_map/pallas_call | solution.py:656
  14.9 1.6 %collective-permute-start.5 = (f32[18,8,256]{2,1,0:T(8,128)S(1)}, f32[18,8,256]{2,1,0:T(8,128)S(1)}, u32[]{:S(2)}, u32[]{:S(2)}) collective-permute-start(f32[18,8,256]{2,1,0:T(8,128)S(1)} %get-tuple-element.105), channel_id=1, source_target_pairs={{0,4},{8,12},{16,20},{24,28},{4,0},{12,8},{20,16},{28,24},{1,5},{9... | collective-permute-start | bytes 442376 | tf_op jit(solution)/shard_map/ppermute | solution.py:642
  16.5 2.3 %collective-permute-start.6 = (f32[18,8,256]{2,1,0:T(8,128)S(1)}, f32[18,8,256]{2,1,0:T(8,128)S(1)}, u32[]{:S(2)}, u32[]{:S(2)}) collective-permute-start(f32[18,8,256]{2,1,0:T(8,128)S(1)} %get-tuple-element.106), channel_id=1, source_target_pairs={{4,8},{12,16},{20,24},{8,4},{16,12},{24,20},{5,9},{13,17},{21,25},... | collective-permute-start | bytes 442376 | tf_op jit(solution)/shard_map/ppermute | solution.py:642
  18.8 0.0 collective-permute-done.3.near
  18.8 0.0 collective-permute-done.4.cross
  18.8 0.0 copy-start
  18.8 0.0 copy-start.1
  18.8 0.0 copy-start.2
  18.8 0.0 copy-start.3
  18.8 0.8 %shard_map.141 = (f32[26,8,256]{2,1,0:T(8,128)S(1)}, f32[26,8,256]{2,1,0:T(8,128)S(1)}, f32[26,8,256]{2,1,0:T(8,128)S(1)}, f32[26,8,256]{2,1,0:T(8,128)S(1)}, f3...) custom-call(f32[24,8,256]{2,1,0:T(8,128)S(1)} %collective-permute-do, ...), custom_call_target="tpu_custom_call" | custom-call | tf_op jit(solution)/shard_map/pallas_call | solution.py:656
  19.7 2.2 %collective-permute-done.5.refs_13_ = f32[18,8,256]{2,1,0:T(8,128)S(1)} collective-permute-done((f32[18,8,256]{2,1,0:T(8,128)S(1)}, f32[18,8,256]{2,1,0:T(8,128)S(1)}, u32[]{:S(2)}, u32[]{:S(2)}) %collective-permute-start.5) | collective-permute-done | bytes 147488 | tf_op jit(solution)/shard_map/ppermute | solution.py:642
  21.9 3.6 %collective-permute-done.6.refs_14_ = f32[18,8,256]{2,1,0:T(8,128)S(1)} collective-permute-done((f32[18,8,256]{2,1,0:T(8,128)S(1)}, f32[18,8,256]{2,1,0:T(8,128)S(1)}, u32[]{:S(2)}, u32[]{:S(2)}) %collective-permute-start.6) | collective-permute-done | bytes 147488 | tf_op jit(solution)/shard_map/ppermute | solution.py:642
  25.4 0.0 copy-done
  25.5 0.0 copy-done.1
  25.5 0.0 copy-done.2
  25.5 0.0 copy-done.3
  25.5 3.9 %shard_map.142 = (f32[16,16,256]{2,1,0:T(8,128)}, f32[16,16,256]{2,1,0:T(8,128)}, f32[16,16,256]{2,1,0:T(8,128)}, f32[16,16,256]{2,1,0:T(8,128)}, f32[1,32]{1,0:...) custom-call(f32[16,16,256]{2,1,0:T(8,128)S(1)} %copy-done, ...), custom_call_target="tpu_custom_call", output_to_operand_aliasing={{5}: (15, {}), {6}: (16, {}), {7}: (17, {}), {8}: (18, {}),... | custom-call | tf_op jit(solution)/shard_map/pallas_call | solution.py:656
  (3 shorter events, 0.0 us)
Async XLA Ops:
  3.1 1.9 %collective-permute-start.1 = (f32[29,16,256]{2,1,0:T(8,128)S(1)}, f32[29,16,256]{2,1,0:T(8,128)S(1)}, u32[]{:S(2)}, u32[]{:S(2)}) collective-permute-start(f32[29,16,256]{2,1,0:T(8,128)S(1)} %get-tuple-element.82), channel_id=1, source_target_pairs={{0,1},{2,3},{1,0},{3,2},{4,5},{6,7},{5,4},{7,6},{8,9},{10,11},{9,8... | collective-permute-start | bytes 1425416 | tf_op jit(solution)/shard_map/ppermute | solution.py:642
  3.1 8.8 %collective-permute-start = (f32[28,16,256]{2,1,0:T(8,128)S(1)}, f32[28,16,256]{2,1,0:T(8,128)S(1)}, u32[]{:S(2)}, u32[]{:S(2)}) collective-permute-start(f32[28,16,256]{2,1,0:T(8,128)S(1)} %get-tuple-element.81), channel_id=1, source_target_pairs={{1,2},{2,1},{5,6},{6,5},{9,10},{10,9},{13,14},{14,13},{17,18},{18,... | collective-permute-start | bytes 1376264 | tf_op jit(solution)/shard_map/ppermute | solution.py:642
  5.0 8.7 %collective-permute-start.2 = (f32[8,128]{1,0:T(8,128)S(1)}, f32[8,128]{1,0:T(8,128)S(1)}, u32[]{:S(2)}, u32[]{:S(2)}) collective-permute-start(f32[8,128]{1,0:T(8,128)S(1)} %pad.4), channel_id=1, source_target_pairs={{0,2},{1,3},{2,0},{3,1},{4,6},{5,7},{6,4},{7,5},{8,10},{9,11},{10,... | collective-permute-start | bytes 12296 | tf_op jit(solution)/shard_map/ppermute | solution.py:740
  8.1 10.6 %collective-permute-start.3 = (f32[24,8,256]{2,1,0:T(8,128)S(1)}, f32[24,8,256]{2,1,0:T(8,128)S(1)}, u32[]{:S(2)}, u32[]{:S(2)}) collective-permute-start(f32[24,8,256]{2,1,0:T(8,128)S(1)} %get-tuple-element.101), channel_id=1, source_target_pairs={{0,4},{8,12},{16,20},{24,28},{4,0},{12,8},{20,16},{28,24},{1,5},{9... | collective-permute-start | bytes 589832 | tf_op jit(solution)/shard_map/ppermute | solution.py:642
  9.7 9.1 %collective-permute-start.4 = (f32[24,8,256]{2,1,0:T(8,128)S(1)}, f32[24,8,256]{2,1,0:T(8,128)S(1)}, u32[]{:S(2)}, u32[]{:S(2)}) collective-permute-start(f32[24,8,256]{2,1,0:T(8,128)S(1)} %get-tuple-element.102), channel_id=1, source_target_pairs={{4,8},{12,16},{20,24},{8,4},{16,12},{24,20},{5,9},{13,17},{21,25},... | collective-permute-start | bytes 589832 | tf_op jit(solution)/shard_map/ppermute | solution.py:642
  14.9 7.0 %collective-permute-start.5 = (f32[18,8,256]{2,1,0:T(8,128)S(1)}, f32[18,8,256]{2,1,0:T(8,128)S(1)}, u32[]{:S(2)}, u32[]{:S(2)}) collective-permute-start(f32[18,8,256]{2,1,0:T(8,128)S(1)} %get-tuple-element.105), channel_id=1, source_target_pairs={{0,4},{8,12},{16,20},{24,28},{4,0},{12,8},{20,16},{28,24},{1,5},{9... | collective-permute-start | bytes 442376 | tf_op jit(solution)/shard_map/ppermute | solution.py:642
  16.5 9.0 %collective-permute-start.6 = (f32[18,8,256]{2,1,0:T(8,128)S(1)}, f32[18,8,256]{2,1,0:T(8,128)S(1)}, u32[]{:S(2)}, u32[]{:S(2)}) collective-permute-start(f32[18,8,256]{2,1,0:T(8,128)S(1)} %get-tuple-element.106), channel_id=1, source_target_pairs={{4,8},{12,16},{20,24},{8,4},{16,12},{24,20},{5,9},{13,17},{21,25},... | collective-permute-start | bytes 442376 | tf_op jit(solution)/shard_map/ppermute | solution.py:642
  18.8 6.7 %copy-start = (f32[16,16,256]{2,1,0:T(8,128)S(1)}, f32[16,16,256]{2,1,0:T(8,128)}, u32[]{:S(2)}) copy-start(f32[16,16,256]{2,1,0:T(8,128)} %refs_0_.1) | copy-start | bytes 786436
  18.8 6.6 %copy-start.1 = (f32[16,16,256]{2,1,0:T(8,128)S(1)}, f32[16,16,256]{2,1,0:T(8,128)}, u32[]{:S(2)}) copy-start(f32[16,16,256]{2,1,0:T(8,128)} %refs_1_.1) | copy-start | bytes 786436
  18.8 6.6 %copy-start.2 = (f32[16,16,256]{2,1,0:T(8,128)S(1)}, f32[16,16,256]{2,1,0:T(8,128)}, u32[]{:S(2)}) copy-start(f32[16,16,256]{2,1,0:T(8,128)} %refs_3_.1) | copy-start | bytes 786436
  18.8 6.6 %copy-start.3 = (f32[16,16,256]{2,1,0:T(8,128)S(1)}, f32[16,16,256]{2,1,0:T(8,128)}, u32[]{:S(2)}) copy-start(f32[16,16,256]{2,1,0:T(8,128)} %refs_2_.1) | copy-start | bytes 786436
where the time goes:
time: 29.7 us; the launch traced here: 29.4 us
  starting transfers between devices  11.6 us (39%)
  Pallas kernels  9.8 us (33%)
  waiting for transfers between devices  7.16 us (24%)
  between operations  0.77 us (3%)
    pallas_call x6, Pallas kernels, call(): pl.pallas_call(kernel, out_shape=[as_struct(s) for s in outs], in_specs=[...  9.8 us
    ppermute x6, starting transfers between devices, swap(): return lax.ppermute(block, axis, pairs + [(b, a) for a, b in pairs])  8.45 us
    ppermute x6, waiting for transfers between devices, swap(): return lax.ppermute(block, axis, pairs + [(b, a) for a, b in pairs])  6.06 us
    ppermute x1, starting transfers between devices, body(): sums = sums + lax.ppermute(tile, 'gz', pairs)[:sums.shape[0]]  3.16 us
    ppermute x1, waiting for transfers between devices, body(): sums = sums + lax.ppermute(tile, 'gz', pairs)[:sums.shape[0]]  1.1 us
  transfers between devices with their start and end apart: 7, of which 4 were waited for; matrix products, arithmetic and copies ran while one was open for 0% of the time, Pallas kernels for 12%

commit v1 on v0

--- a/solution.py
+++ b/solution.py
@@ -47,19 +47,22 @@
     top = H + layers
     both = lambda name, n: ((name, H - n, n), (name, top, n))
     faces = lambda name, n: ((name, H - n, n), (name, top - 1, n))
+    ends = lambda name: ((name, 2, 1), (name, top + 2, 1))
     return (
-        ("rhs", 2, layers + 6),
+        ("rhs", 3, layers + 4),
+        *ends("rhs_x"),
         ("p1_d2", 3, layers + 4),
         ("g2", 4, layers + 2),
         ("g3", H, layers),
         *both("t1", H - 1),
         *both("tot", H - 1),
         *both("p0", H - 1),
-        *both("dp", H - 2),
-        *faces("f0", H - 1),
-        *both("f2", H - 2),
-        *both("f1", H - 2),
-        *both("p0_d2", H - 2),
+        *both("dp", H - 3),
+        *ends("dp_x"),
+        *faces("f0", H - 2),
+        *both("f2", H - 3),
+        *both("f1", H - 3),
+        *both("p0_d2", H - 3),
         *faces("f0_d2", 2),
         *both("f2_d2", 1),
         *both("dp_d2", 1),
@@ -86,6 +89,8 @@
     "p0_d2": ("p0", 1, 6),
     "p1_d2": ("p1", 1, 6),
     "rhs": ("rhs2", 0, 7),
+    "rhs_x": ("rhs2", 0, 7),
+    "dp_x": ("dp", 0, 7),
     "g2": ("rhs2", 1, 6),
     "g3": ("rhs3", 1, 6),
 }
@@ -515,7 +520,8 @@
 
 def build_kernel(*refs, layers, gx):
     p0e, stor, f0e, f1e, f2e, dpe, tote, base, inverse, sums, perfs, hot, own_hot = refs[:13]
-    cell, wells, rhse, source, x_near, x_cross, bottom, p1, g2u, g2d, g3u, g3d = refs[13:]
+    cell, wells, rhse, source, x_near, x_cross, bottom = refs[13:20]
+    p1, g2u, g2d, g3u, g3d, rxu, rxd, dpx = refs[20:]
     ext, rows, columns = p0e.shape
     last_row, _ = masks(rows, columns)
     hole = well_holes(sums[...], wells[...])
@@ -566,10 +572,21 @@
 
     loop(H - 1, ext - H + 1, second_step, 0)
 
+    for e, beside, face in ((2, 1, 1), (ext - 3, ext - 2, ext - 3)):
+        along = jnp.where(last_row, 0.0, f1e[e])
+        across = f2e[e]
+        p = p0e[e]
+        rhs = rhse[e] + f0e[face] * p0e[beside]
+        rhs = rhs + across * roll(p, -1, 1) + roll(across * p, 1, 1)
+        rxu[e] = rhs + roll(along * p, 1, 0)
+        rxd[e] = rhs + along * roll(p, -1, 0)
+        dpx[e] = dpe[e] + f0e[face]
+
     shared = {"t1": f1e, "tot": tote, "p0": p0e, "dp": dpe, "f0": f0e, "f2": f2e, "f1": f1e}
     shared |= {"p0_d2": p0e, "f0_d2": f0e, "f2_d2": f2e, "dp_d2": dpe, "rhs": rhse, "p1_d2": p1}
-    up = shared | {"g2": g2u, "g3": g3u}
-    down = shared | {"g2": g2d, "g3": g3d}
+    shared["dp_x"] = dpx
+    up = shared | {"g2": g2u, "g3": g3u, "rhs_x": rxu}
+    down = shared | {"g2": g2d, "g3": g3d, "rhs_x": rxd}
     pack_both(x_near, x_cross, late_parts(layers), up, down, rows, gx)
 
 
@@ -765,7 +782,7 @@
     rhse, source, late_near, late_cross, hole = call(
         functools.partial(build_kernel, layers=layers, gx="gx"),
         [ext_block, pinned, late, late, pin(1, LANES)],
-        [ext_block] * 5,
+        [ext_block] * 8,
         p0e,
         stor,
         f0e,

time: 29.7 us -> 29.4 us (0.990)
  no operation moved by 1% of the time
where the time goes in v1:
time: 29.4 us; the launch traced here: 29.3 us
  starting transfers between devices  11.6 us (39%)
  Pallas kernels  9.84 us (33%)
  waiting for transfers between devices  7 us (24%)
  between operations  0.77 us (3%)
    pallas_call x6, Pallas kernels, call(): pl.pallas_call(kernel, out_shape=[as_struct(s) for s in outs], in_specs=[...  9.84 us
    ppermute x6, starting transfers between devices, swap(): return lax.ppermute(block, axis, pairs + [(b, a) for a, b in pairs])  8.45 us
    ppermute x6, waiting for transfers between devices, swap(): return lax.ppermute(block, axis, pairs + [(b, a) for a, b in pairs])  5.9 us
    ppermute x1, starting transfers between devices, body(): sums = sums + lax.ppermute(tile, 'gz', pairs)[:sums.shape[0]]  3.16 us
    ppermute x1, waiting for transfers between devices, body(): sums = sums + lax.ppermute(tile, 'gz', pairs)[:sums.shape[0]]  1.1 us
  transfers between devices with their start and end apart: 7, of which 4 were waited for; matrix products, arithmetic and copies ran while one was open for 0% of the time, Pallas kernels for 12%

profile of v1, /device:TPU:24, one launch (start us, length us, event | category | flops | bytes accessed | tf_op | source)
XLA Modules:
  0.0 29.3 jit_solution(947981323177651579)
XLA Ops:
  0.6 2.4 %shard_map.137 = (f32[26,16,256]{2,1,0:T(8,128)S(1)}, f32[26,16,256]{2,1,0:T(8,128)S(1)}, f32[26,16,256]{2,1,0:T(8,128)S(1)}, f32[26,16,256]{2,1,0:T(8,128)S(1)}...) custom-call(f32[16,16,256]{2,1,0:T(8,128)} %refs_0_.1, ...), custom_call_target="tpu_custom_call" | custom-call | tf_op jit(solution)/shard_map/pallas_call | solution.py:673
  3.1 0.1 collective-permute-start.1
  3.1 0.7 %collective-permute-start = (f32[28,16,256]{2,1,0:T(8,128)S(1)}, f32[28,16,256]{2,1,0:T(8,128)S(1)}, u32[]{:S(2)}, u32[]{:S(2)}) collective-permute-start(f32[28,16,256]{2,1,0:T(8,128)S(1)} %get-tuple-element.81), channel_id=1, source_target_pairs={{1,2},{2,1},{5,6},{6,5},{9,10},{10,9},{13,14},{14,13},{17,18},{18,... | collective-permute-start | bytes 1376264 | tf_op jit(solution)/shard_map/ppermute | solution.py:659
  3.8 0.9 %shard_map.138 = (f32[26,16,256]{2,1,0:T(8,128)S(1)}, f32[26,16,256]{2,1,0:T(8,128)S(1)}, f32[26,16,256]{2,1,0:T(8,128)S(1)}, f32[26,16,256]{2,1,0:T(8,128)S(1)}...) custom-call(f32[26,16,256]{2,1,0:T(8,128)S(1)} %get-tuple-element.67, ...), custom_call_target="tpu_custom_call" | custom-call | tf_op jit(solution)/shard_map/pallas_call | solution.py:673
  4.7 0.3 collective-permute-done.1.refs_12_
  5.0 3.2 %collective-permute-start.2 = (f32[8,128]{1,0:T(8,128)S(1)}, f32[8,128]{1,0:T(8,128)S(1)}, u32[]{:S(2)}, u32[]{:S(2)}) collective-permute-start(f32[8,128]{1,0:T(8,128)S(1)} %pad.4), channel_id=1, source_target_pairs={{0,2},{1,3},{2,0},{3,1},{4,6},{5,7},{6,4},{7,5},{8,10},{9,11},{10,... | collective-permute-start | bytes 12296 | tf_op jit(solution)/shard_map/ppermute | solution.py:757
  8.1 1.5 %collective-permute-start.3 = (f32[24,8,256]{2,1,0:T(8,128)S(1)}, f32[24,8,256]{2,1,0:T(8,128)S(1)}, u32[]{:S(2)}, u32[]{:S(2)}) collective-permute-start(f32[24,8,256]{2,1,0:T(8,128)S(1)} %get-tuple-element.101), channel_id=1, source_target_pairs={{0,4},{8,12},{16,20},{24,28},{4,0},{12,8},{20,16},{28,24},{1,5},{9... | collective-permute-start | bytes 589832 | tf_op jit(solution)/shard_map/ppermute | solution.py:659
  9.7 2.3 %collective-permute-start.4 = (f32[24,8,256]{2,1,0:T(8,128)S(1)}, f32[24,8,256]{2,1,0:T(8,128)S(1)}, u32[]{:S(2)}, u32[]{:S(2)}) collective-permute-start(f32[24,8,256]{2,1,0:T(8,128)S(1)} %get-tuple-element.102), channel_id=1, source_target_pairs={{4,8},{12,16},{20,24},{8,4},{16,12},{24,20},{5,9},{13,17},{21,25},... | collective-permute-start | bytes 589832 | tf_op jit(solution)/shard_map/ppermute | solution.py:659
  12.0 0.0 collective-permute-done.refs_11_
  12.0 0.6 %shard_map.139 = (f32[26,16,256]{2,1,0:T(8,128)S(1)}, f32[26,16,256]{2,1,0:T(8,128)S(1)}, f32[26,16,256]{2,1,0:T(8,128)S(1)}, f32[26,16,256]{2,1,0:T(8,128)S(1)}...) custom-call(f32[26,16,256]{2,1,0:T(8,128)S(1)} %get-tuple-element.67, ...), custom_call_target="tpu_custom_call", output_to_operand_aliasing={{0}: (0, {}), {1}: (1, {}), {2}: (2, {}), {3}: (3, {}), {4}... | custom-call | tf_op jit(solution)/shard_map/pallas_call | solution.py:673
  12.6 1.1 %collective-permute-done.2 = f32[8,128]{1,0:T(8,128)S(1)} collective-permute-done((f32[8,128]{1,0:T(8,128)S(1)}, f32[8,128]{1,0:T(8,128)S(1)}, u32[]{:S(2)}, u32[]{:S(2)}) %collective-permute-start.2) | collective-permute-done | bytes 4128 | tf_op jit(solution)/shard_map/ppermute | solution.py:757
  13.7 1.2 %shard_map.140 = (f32[26,16,256]{2,1,0:T(8,128)S(1)}, f32[16,16,256]{2,1,0:T(8,128)S(1)}, f32[17,8,256]{2,1,0:T(8,128)S(1)}, f32[17,8,256]{2,1,0:T(8,128)S(1)}, f32[1,128]{1,0:T(1,128)S(1)}) custom-call(f32[26,16,256]{2,1,0:T(8,128)S(1)} %get-tuple-element.86.refs_0_.refs_5_, f32[26,16,256]{2,1,0:T(8,128)S(1)} %get-tuple-element.87.refs_1_, ...), custom_call_target="tpu_custom_call" | custom-call | tf_op jit(solution)/shard_map/pallas_call | solution.py:673
  14.9 1.6 %collective-permute-start.5 = (f32[17,8,256]{2,1,0:T(8,128)S(1)}, f32[17,8,256]{2,1,0:T(8,128)S(1)}, u32[]{:S(2)}, u32[]{:S(2)}) collective-permute-start(f32[17,8,256]{2,1,0:T(8,128)S(1)} %get-tuple-element.105), channel_id=1, source_target_pairs={{0,4},{8,12},{16,20},{24,28},{4,0},{12,8},{20,16},{28,24},{1,5},{9... | collective-permute-start | bytes 417800 | tf_op jit(solution)/shard_map/ppermute | solution.py:659
  16.5 2.3 %collective-permute-start.6 = (f32[17,8,256]{2,1,0:T(8,128)S(1)}, f32[17,8,256]{2,1,0:T(8,128)S(1)}, u32[]{:S(2)}, u32[]{:S(2)}) collective-permute-start(f32[17,8,256]{2,1,0:T(8,128)S(1)} %get-tuple-element.106), channel_id=1, source_target_pairs={{4,8},{12,16},{20,24},{8,4},{16,12},{24,20},{5,9},{13,17},{21,25},... | collective-permute-start | bytes 417800 | tf_op jit(solution)/shard_map/ppermute | solution.py:659
  18.8 0.0 collective-permute-done.3.near
  18.8 0.0 collective-permute-done.4.cross
  18.8 0.0 copy-start
  18.9 0.0 copy-start.1
  18.9 0.0 copy-start.2
  18.9 0.0 copy-start.3
  18.9 0.8 %shard_map.141 = (f32[26,8,256]{2,1,0:T(8,128)S(1)}, f32[26,8,256]{2,1,0:T(8,128)S(1)}, f32[26,8,256]{2,1,0:T(8,128)S(1)}, f32[26,8,256]{2,1,0:T(8,128)S(1)}, f3...) custom-call(f32[24,8,256]{2,1,0:T(8,128)S(1)} %collective-permute-do, ...), custom_call_target="tpu_custom_call" | custom-call | tf_op jit(solution)/shard_map/pallas_call | solution.py:673
  19.7 2.0 %collective-permute-done.5.refs_13_ = f32[17,8,256]{2,1,0:T(8,128)S(1)} collective-permute-done((f32[17,8,256]{2,1,0:T(8,128)S(1)}, f32[17,8,256]{2,1,0:T(8,128)S(1)}, u32[]{:S(2)}, u32[]{:S(2)}) %collective-permute-start.5) | collective-permute-done | bytes 139296 | tf_op jit(solution)/shard_map/ppermute | solution.py:659
  21.7 3.6 %collective-permute-done.6.refs_14_ = f32[17,8,256]{2,1,0:T(8,128)S(1)} collective-permute-done((f32[17,8,256]{2,1,0:T(8,128)S(1)}, f32[17,8,256]{2,1,0:T(8,128)S(1)}, u32[]{:S(2)}, u32[]{:S(2)}) %collective-permute-start.6) | collective-permute-done | bytes 139296 | tf_op jit(solution)/shard_map/ppermute | solution.py:659
  25.3 0.0 copy-done
  25.3 0.0 copy-done.1
  25.3 0.0 copy-done.2
  25.3 0.0 copy-done.3
  25.4 3.9 %shard_map.142 = (f32[16,16,256]{2,1,0:T(8,128)}, f32[16,16,256]{2,1,0:T(8,128)}, f32[16,16,256]{2,1,0:T(8,128)}, f32[16,16,256]{2,1,0:T(8,128)}, f32[1,32]{1,0:...) custom-call(f32[16,16,256]{2,1,0:T(8,128)S(1)} %copy-done, ...), custom_call_target="tpu_custom_call", output_to_operand_aliasing={{5}: (15, {}), {6}: (16, {}), {7}: (17, {}), {8}: (18, {}),... | custom-call | tf_op jit(solution)/shard_map/pallas_call | solution.py:673
  (3 shorter events, 0.0 us)
Async XLA Ops:
  3.1 1.9 %collective-permute-start.1 = (f32[29,16,256]{2,1,0:T(8,128)S(1)}, f32[29,16,256]{2,1,0:T(8,128)S(1)}, u32[]{:S(2)}, u32[]{:S(2)}) collective-permute-start(f32[29,16,256]{2,1,0:T(8,128)S(1)} %get-tuple-element.82), channel_id=1, source_target_pairs={{0,1},{2,3},{1,0},{3,2},{4,5},{6,7},{5,4},{7,6},{8,9},{10,11},{9,8... | collective-permute-start | bytes 1425416 | tf_op jit(solution)/shard_map/ppermute | solution.py:659
  3.1 8.8 %collective-permute-start = (f32[28,16,256]{2,1,0:T(8,128)S(1)}, f32[28,16,256]{2,1,0:T(8,128)S(1)}, u32[]{:S(2)}, u32[]{:S(2)}) collective-permute-start(f32[28,16,256]{2,1,0:T(8,128)S(1)} %get-tuple-element.81), channel_id=1, source_target_pairs={{1,2},{2,1},{5,6},{6,5},{9,10},{10,9},{13,14},{14,13},{17,18},{18,... | collective-permute-start | bytes 1376264 | tf_op jit(solution)/shard_map/ppermute | solution.py:659
  5.0 8.7 %collective-permute-start.2 = (f32[8,128]{1,0:T(8,128)S(1)}, f32[8,128]{1,0:T(8,128)S(1)}, u32[]{:S(2)}, u32[]{:S(2)}) collective-permute-start(f32[8,128]{1,0:T(8,128)S(1)} %pad.4), channel_id=1, source_target_pairs={{0,2},{1,3},{2,0},{3,1},{4,6},{5,7},{6,4},{7,5},{8,10},{9,11},{10,... | collective-permute-start | bytes 12296 | tf_op jit(solution)/shard_map/ppermute | solution.py:757
  8.1 10.7 %collective-permute-start.3 = (f32[24,8,256]{2,1,0:T(8,128)S(1)}, f32[24,8,256]{2,1,0:T(8,128)S(1)}, u32[]{:S(2)}, u32[]{:S(2)}) collective-permute-start(f32[24,8,256]{2,1,0:T(8,128)S(1)} %get-tuple-element.101), channel_id=1, source_target_pairs={{0,4},{8,12},{16,20},{24,28},{4,0},{12,8},{20,16},{28,24},{1,5},{9... | collective-permute-start | bytes 589832 | tf_op jit(solution)/shard_map/ppermute | solution.py:659
  9.7 9.2 %collective-permute-start.4 = (f32[24,8,256]{2,1,0:T(8,128)S(1)}, f32[24,8,256]{2,1,0:T(8,128)S(1)}, u32[]{:S(2)}, u32[]{:S(2)}) collective-permute-start(f32[24,8,256]{2,1,0:T(8,128)S(1)} %get-tuple-element.102), channel_id=1, source_target_pairs={{4,8},{12,16},{20,24},{8,4},{16,12},{24,20},{5,9},{13,17},{21,25},... | collective-permute-start | bytes 589832 | tf_op jit(solution)/shard_map/ppermute | solution.py:659
  14.9 6.8 %collective-permute-start.5 = (f32[17,8,256]{2,1,0:T(8,128)S(1)}, f32[17,8,256]{2,1,0:T(8,128)S(1)}, u32[]{:S(2)}, u32[]{:S(2)}) collective-permute-start(f32[17,8,256]{2,1,0:T(8,128)S(1)} %get-tuple-element.105), channel_id=1, source_target_pairs={{0,4},{8,12},{16,20},{24,28},{4,0},{12,8},{20,16},{28,24},{1,5},{9... | collective-permute-start | bytes 417800 | tf_op jit(solution)/shard_map/ppermute | solution.py:659
  16.5 8.8 %collective-permute-start.6 = (f32[17,8,256]{2,1,0:T(8,128)S(1)}, f32[17,8,256]{2,1,0:T(8,128)S(1)}, u32[]{:S(2)}, u32[]{:S(2)}) collective-permute-start(f32[17,8,256]{2,1,0:T(8,128)S(1)} %get-tuple-element.106), channel_id=1, source_target_pairs={{4,8},{12,16},{20,24},{8,4},{16,12},{24,20},{5,9},{13,17},{21,25},... | collective-permute-start | bytes 417800 | tf_op jit(solution)/shard_map/ppermute | solution.py:659
  18.8 6.5 %copy-start = (f32[16,16,256]{2,1,0:T(8,128)S(1)}, f32[16,16,256]{2,1,0:T(8,128)}, u32[]{:S(2)}) copy-start(f32[16,16,256]{2,1,0:T(8,128)} %refs_0_.1) | copy-start | bytes 786436
  18.9 6.5 %copy-start.1 = (f32[16,16,256]{2,1,0:T(8,128)S(1)}, f32[16,16,256]{2,1,0:T(8,128)}, u32[]{:S(2)}) copy-start(f32[16,16,256]{2,1,0:T(8,128)} %refs_1_.1) | copy-start | bytes 786436
  18.9 6.5 %copy-start.2 = (f32[16,16,256]{2,1,0:T(8,128)S(1)}, f32[16,16,256]{2,1,0:T(8,128)}, u32[]{:S(2)}) copy-start(f32[16,16,256]{2,1,0:T(8,128)} %refs_3_.1) | copy-start | bytes 786436
  18.9 6.5 %copy-start.3 = (f32[16,16,256]{2,1,0:T(8,128)S(1)}, f32[16,16,256]{2,1,0:T(8,128)}, u32[]{:S(2)}) copy-start(f32[16,16,256]{2,1,0:T(8,128)} %refs_2_.1) | copy-start | bytes 786436

commit v2 on v1

--- a/solution.py
+++ b/solution.py
@@ -756,6 +756,7 @@
         tile = jnp.pad(sums, ((0, 8 - sums.shape[0]), (0, 0)))
         sums = sums + lax.ppermute(tile, "gz", pairs)[: sums.shape[0]]
         step *= 2
+    early_near, near = lax.optimization_barrier((early_near, near))
     p0e, tote, frace, stor, f0e, f1e, f2e, dpe, base, inverse, perf_values, hot = call(
         functools.partial(halo_kernel, layers=layers, gx="gx", gz="gz"),
         [ext_block] * 10

time: 29.4 us -> 29.2 us (level)
  waiting for transfers between devices: 7 us -> 6.41 us
  starting transfers between devices: 11.6 us -> 11.9 us
    ppermute x6, waiting for transfers between devices: 5.9 us -> 5.37 us  [swap(): return lax.ppermute(block, axis, pairs + [(b, a) for a, b in pairs])]
  transfers between devices with their start and end apart: 7 -> 7, of which waited for: 4 -> 3; matrix products, arithmetic and copies ran while one was open for 0% -> 0% of each run, Pallas kernels for 12% -> 12%
where the time goes in v2:
time: 29.2 us; the launch traced here: 29 us
  starting transfers between devices  11.9 us (41%)
  Pallas kernels  9.83 us (34%)
  waiting for transfers between devices  6.41 us (22%)
  between operations  0.77 us (3%)
    pallas_call x6, Pallas kernels, call(): pl.pallas_call(kernel, out_shape=[as_struct(s) for s in outs], in_specs=[...  9.83 us
    ppermute x6, starting transfers between devices, swap(): return lax.ppermute(block, axis, pairs + [(b, a) for a, b in pairs])  8.51 us
    ppermute x6, waiting for transfers between devices, swap(): return lax.ppermute(block, axis, pairs + [(b, a) for a, b in pairs])  5.37 us
    ppermute x1, starting transfers between devices, body(): sums = sums + lax.ppermute(tile, 'gz', pairs)[:sums.shape[0]]  3.4 us
    ppermute x1, waiting for transfers between devices, body(): sums = sums + lax.ppermute(tile, 'gz', pairs)[:sums.shape[0]]  1.05 us
  transfers between devices with their start and end apart: 7, of which 3 were waited for; matrix products, arithmetic and copies ran while one was open for 0% of the time, Pallas kernels for 12%

profile of v2, /device:TPU:24, one launch (start us, length us, event | category | flops | bytes accessed | tf_op | source)
XLA Modules:
  0.0 29.0 jit_solution(13556380068612914156)
XLA Ops:
  0.6 2.4 %shard_map.137 = (f32[26,16,256]{2,1,0:T(8,128)S(1)}, f32[26,16,256]{2,1,0:T(8,128)S(1)}, f32[26,16,256]{2,1,0:T(8,128)S(1)}, f32[26,16,256]{2,1,0:T(8,128)S(1)}...) custom-call(f32[16,16,256]{2,1,0:T(8,128)} %refs_0_.1, ...), custom_call_target="tpu_custom_call" | custom-call | tf_op jit(solution)/shard_map/pallas_call | solution.py:673
  3.1 0.1 collective-permute-start.2
  3.1 0.7 %collective-permute-start = (f32[28,16,256]{2,1,0:T(8,128)S(1)}, f32[28,16,256]{2,1,0:T(8,128)S(1)}, u32[]{:S(2)}, u32[]{:S(2)}) collective-permute-start(f32[28,16,256]{2,1,0:T(8,128)S(1)} %get-tuple-element.83), channel_id=1, source_target_pairs={{1,2},{2,1},{5,6},{6,5},{9,10},{10,9},{13,14},{14,13},{17,18},{18,... | collective-permute-start | bytes 1376264 | tf_op jit(solution)/shard_map/ppermute | solution.py:659
  3.8 0.9 %shard_map.138 = (f32[26,16,256]{2,1,0:T(8,128)S(1)}, f32[26,16,256]{2,1,0:T(8,128)S(1)}, f32[26,16,256]{2,1,0:T(8,128)S(1)}, f32[26,16,256]{2,1,0:T(8,128)S(1)}...) custom-call(f32[26,16,256]{2,1,0:T(8,128)S(1)} %get-tuple-element.69, ...), custom_call_target="tpu_custom_call" | custom-call | tf_op jit(solution)/shard_map/pallas_call | solution.py:673
  4.7 1.6 %collective-permute-start.1 = (f32[24,8,256]{2,1,0:T(8,128)S(1)}, f32[24,8,256]{2,1,0:T(8,128)S(1)}, u32[]{:S(2)}, u32[]{:S(2)}) collective-permute-start(f32[24,8,256]{2,1,0:T(8,128)S(1)} %get-tuple-element.84), channel_id=1, source_target_pairs={{0,4},{8,12},{16,20},{24,28},{4,0},{12,8},{20,16},{28,24},{1,5},{9... | collective-permute-start | bytes 589832 | tf_op jit(solution)/shard_map/ppermute | solution.py:659
  6.3 0.0 collective-permute-done.2.refs_12_
  6.3 3.4 %collective-permute-start.3 = (f32[8,128]{1,0:T(8,128)S(1)}, f32[8,128]{1,0:T(8,128)S(1)}, u32[]{:S(2)}, u32[]{:S(2)}) collective-permute-start(f32[8,128]{1,0:T(8,128)S(1)} %pad.4), channel_id=1, source_target_pairs={{0,2},{1,3},{2,0},{3,1},{4,6},{5,7},{6,4},{7,5},{8,10},{9,11},{10,... | collective-permute-start | bytes 12296 | tf_op jit(solution)/shard_map/ppermute | solution.py:757
  9.7 2.3 %collective-permute-start.4 = (f32[24,8,256]{2,1,0:T(8,128)S(1)}, f32[24,8,256]{2,1,0:T(8,128)S(1)}, u32[]{:S(2)}, u32[]{:S(2)}) collective-permute-start(f32[24,8,256]{2,1,0:T(8,128)S(1)} %get-tuple-element.106), channel_id=1, source_target_pairs={{4,8},{12,16},{20,24},{8,4},{16,12},{24,20},{5,9},{13,17},{21,25},... | collective-permute-start | bytes 589832 | tf_op jit(solution)/shard_map/ppermute | solution.py:659
  12.0 0.0 collective-permute-done.1.near
  12.0 0.0 collective-permute-done.refs_11_
  12.0 0.6 %shard_map.139 = (f32[26,16,256]{2,1,0:T(8,128)S(1)}, f32[26,16,256]{2,1,0:T(8,128)S(1)}, f32[26,16,256]{2,1,0:T(8,128)S(1)}, f32[26,16,256]{2,1,0:T(8,128)S(1)}...) custom-call(f32[26,16,256]{2,1,0:T(8,128)S(1)} %get-tuple-element.69, ...), custom_call_target="tpu_custom_call", output_to_operand_aliasing={{0}: (0, {}), {1}: (1, {}), {2}: (2, {}), {3}: (3, {}), {4}... | custom-call | tf_op jit(solution)/shard_map/pallas_call | solution.py:673
  12.6 1.0 %collective-permute-done.3 = f32[8,128]{1,0:T(8,128)S(1)} collective-permute-done((f32[8,128]{1,0:T(8,128)S(1)}, f32[8,128]{1,0:T(8,128)S(1)}, u32[]{:S(2)}, u32[]{:S(2)}) %collective-permute-start.3) | collective-permute-done | bytes 4128 | tf_op jit(solution)/shard_map/ppermute | solution.py:757
  13.7 1.2 %shard_map.140 = (f32[26,16,256]{2,1,0:T(8,128)S(1)}, f32[16,16,256]{2,1,0:T(8,128)S(1)}, f32[17,8,256]{2,1,0:T(8,128)S(1)}, f32[17,8,256]{2,1,0:T(8,128)S(1)}, f32[1,128]{1,0:T(1,128)S(1)}) custom-call(f32[26,16,256]{2,1,0:T(8,128)S(1)} %get-tuple-element.90.refs_0_.refs_5_, f32[26,16,256]{2,1,0:T(8,128)S(1)} %get-tuple-element.91.refs_1_, ...), custom_call_target="tpu_custom_call" | custom-call | tf_op jit(solution)/shard_map/pallas_call | solution.py:673
  14.9 1.6 %collective-permute-start.5 = (f32[17,8,256]{2,1,0:T(8,128)S(1)}, f32[17,8,256]{2,1,0:T(8,128)S(1)}, u32[]{:S(2)}, u32[]{:S(2)}) collective-permute-start(f32[17,8,256]{2,1,0:T(8,128)S(1)} %get-tuple-element.109), channel_id=1, source_target_pairs={{0,4},{8,12},{16,20},{24,28},{4,0},{12,8},{20,16},{28,24},{1,5},{9... | collective-permute-start | bytes 417800 | tf_op jit(solution)/shard_map/ppermute | solution.py:659
  16.5 2.3 %collective-permute-start.6 = (f32[17,8,256]{2,1,0:T(8,128)S(1)}, f32[17,8,256]{2,1,0:T(8,128)S(1)}, u32[]{:S(2)}, u32[]{:S(2)}) collective-permute-start(f32[17,8,256]{2,1,0:T(8,128)S(1)} %get-tuple-element.110), channel_id=1, source_target_pairs={{4,8},{12,16},{20,24},{8,4},{16,12},{24,20},{5,9},{13,17},{21,25},... | collective-permute-start | bytes 417800 | tf_op jit(solution)/shard_map/ppermute | solution.py:659
  18.8 0.0 collective-permute-done.4.cross
  18.8 0.0 copy-start
  18.8 0.0 copy-start.1
  18.9 0.0 copy-start.2
  18.9 0.0 copy-start.3
  18.9 0.8 %shard_map.141 = (f32[26,8,256]{2,1,0:T(8,128)S(1)}, f32[26,8,256]{2,1,0:T(8,128)S(1)}, f32[26,8,256]{2,1,0:T(8,128)S(1)}, f32[26,8,256]{2,1,0:T(8,128)S(1)}, f3...) custom-call(f32[24,8,256]{2,1,0:T(8,128)S(1)} %collective-permute-do, ...), custom_call_target="tpu_custom_call" | custom-call | tf_op jit(solution)/shard_map/pallas_call | solution.py:673
  19.7 1.8 %collective-permute-done.5.refs_13_ = f32[17,8,256]{2,1,0:T(8,128)S(1)} collective-permute-done((f32[17,8,256]{2,1,0:T(8,128)S(1)}, f32[17,8,256]{2,1,0:T(8,128)S(1)}, u32[]{:S(2)}, u32[]{:S(2)}) %collective-permute-start.5) | collective-permute-done | bytes 139296 | tf_op jit(solution)/shard_map/ppermute | solution.py:659
  21.5 3.5 %collective-permute-done.6.refs_14_ = f32[17,8,256]{2,1,0:T(8,128)S(1)} collective-permute-done((f32[17,8,256]{2,1,0:T(8,128)S(1)}, f32[17,8,256]{2,1,0:T(8,128)S(1)}, u32[]{:S(2)}, u32[]{:S(2)}) %collective-permute-start.6) | collective-permute-done | bytes 139296 | tf_op jit(solution)/shard_map/ppermute | solution.py:659
  25.0 0.0 copy-done
  25.0 0.0 copy-done.1
  25.0 0.0 copy-done.2
  25.1 0.0 copy-done.3
  25.1 3.9 %shard_map.142 = (f32[16,16,256]{2,1,0:T(8,128)}, f32[16,16,256]{2,1,0:T(8,128)}, f32[16,16,256]{2,1,0:T(8,128)}, f32[16,16,256]{2,1,0:T(8,128)}, f32[1,32]{1,0:...) custom-call(f32[16,16,256]{2,1,0:T(8,128)S(1)} %copy-done, ...), custom_call_target="tpu_custom_call", output_to_operand_aliasing={{5}: (15, {}), {6}: (16, {}), {7}: (17, {}), {8}: (18, {}),... | custom-call | tf_op jit(solution)/shard_map/pallas_call | solution.py:673
  (3 shorter events, 0.0 us)
Async XLA Ops:
  3.1 3.2 %collective-permute-start.2 = (f32[29,16,256]{2,1,0:T(8,128)S(1)}, f32[29,16,256]{2,1,0:T(8,128)S(1)}, u32[]{:S(2)}, u32[]{:S(2)}) collective-permute-start(f32[29,16,256]{2,1,0:T(8,128)S(1)} %get-tuple-element.85), channel_id=1, source_target_pairs={{0,1},{2,3},{1,0},{3,2},{4,5},{6,7},{5,4},{7,6},{8,9},{10,11},{9,8... | collective-permute-start | bytes 1425416 | tf_op jit(solution)/shard_map/ppermute | solution.py:659
  3.1 8.9 %collective-permute-start = (f32[28,16,256]{2,1,0:T(8,128)S(1)}, f32[28,16,256]{2,1,0:T(8,128)S(1)}, u32[]{:S(2)}, u32[]{:S(2)}) collective-permute-start(f32[28,16,256]{2,1,0:T(8,128)S(1)} %get-tuple-element.83), channel_id=1, source_target_pairs={{1,2},{2,1},{5,6},{6,5},{9,10},{10,9},{13,14},{14,13},{17,18},{18,... | collective-permute-start | bytes 1376264 | tf_op jit(solution)/shard_map/ppermute | solution.py:659
  4.7 7.3 %collective-permute-start.1 = (f32[24,8,256]{2,1,0:T(8,128)S(1)}, f32[24,8,256]{2,1,0:T(8,128)S(1)}, u32[]{:S(2)}, u32[]{:S(2)}) collective-permute-start(f32[24,8,256]{2,1,0:T(8,128)S(1)} %get-tuple-element.84), channel_id=1, source_target_pairs={{0,4},{8,12},{16,20},{24,28},{4,0},{12,8},{20,16},{28,24},{1,5},{9... | collective-permute-start | bytes 589832 | tf_op jit(solution)/shard_map/ppermute | solution.py:659
  6.3 7.4 %collective-permute-start.3 = (f32[8,128]{1,0:T(8,128)S(1)}, f32[8,128]{1,0:T(8,128)S(1)}, u32[]{:S(2)}, u32[]{:S(2)}) collective-permute-start(f32[8,128]{1,0:T(8,128)S(1)} %pad.4), channel_id=1, source_target_pairs={{0,2},{1,3},{2,0},{3,1},{4,6},{5,7},{6,4},{7,5},{8,10},{9,11},{10,... | collective-permute-start | bytes 12296 | tf_op jit(solution)/shard_map/ppermute | solution.py:757
  9.7 9.1 %collective-permute-start.4 = (f32[24,8,256]{2,1,0:T(8,128)S(1)}, f32[24,8,256]{2,1,0:T(8,128)S(1)}, u32[]{:S(2)}, u32[]{:S(2)}) collective-permute-start(f32[24,8,256]{2,1,0:T(8,128)S(1)} %get-tuple-element.106), channel_id=1, source_target_pairs={{4,8},{12,16},{20,24},{8,4},{16,12},{24,20},{5,9},{13,17},{21,25},... | collective-permute-start | bytes 589832 | tf_op jit(solution)/shard_map/ppermute | solution.py:659
  14.9 6.6 %collective-permute-start.5 = (f32[17,8,256]{2,1,0:T(8,128)S(1)}, f32[17,8,256]{2,1,0:T(8,128)S(1)}, u32[]{:S(2)}, u32[]{:S(2)}) collective-permute-start(f32[17,8,256]{2,1,0:T(8,128)S(1)} %get-tuple-element.109), channel_id=1, source_target_pairs={{0,4},{8,12},{16,20},{24,28},{4,0},{12,8},{20,16},{28,24},{1,5},{9... | collective-permute-start | bytes 417800 | tf_op jit(solution)/shard_map/ppermute | solution.py:659
  16.5 8.5 %collective-permute-start.6 = (f32[17,8,256]{2,1,0:T(8,128)S(1)}, f32[17,8,256]{2,1,0:T(8,128)S(1)}, u32[]{:S(2)}, u32[]{:S(2)}) collective-permute-start(f32[17,8,256]{2,1,0:T(8,128)S(1)} %get-tuple-element.110), channel_id=1, source_target_pairs={{4,8},{12,16},{20,24},{8,4},{16,12},{24,20},{5,9},{13,17},{21,25},... | collective-permute-start | bytes 417800 | tf_op jit(solution)/shard_map/ppermute | solution.py:659
  18.8 6.2 %copy-start = (f32[16,16,256]{2,1,0:T(8,128)S(1)}, f32[16,16,256]{2,1,0:T(8,128)}, u32[]{:S(2)}) copy-start(f32[16,16,256]{2,1,0:T(8,128)} %refs_0_.1) | copy-start | bytes 786436
  18.8 6.2 %copy-start.1 = (f32[16,16,256]{2,1,0:T(8,128)S(1)}, f32[16,16,256]{2,1,0:T(8,128)}, u32[]{:S(2)}) copy-start(f32[16,16,256]{2,1,0:T(8,128)} %refs_1_.1) | copy-start | bytes 786436
  18.9 6.2 %copy-start.2 = (f32[16,16,256]{2,1,0:T(8,128)S(1)}, f32[16,16,256]{2,1,0:T(8,128)}, u32[]{:S(2)}) copy-start(f32[16,16,256]{2,1,0:T(8,128)} %refs_3_.1) | copy-start | bytes 786436
  18.9 6.2 %copy-start.3 = (f32[16,16,256]{2,1,0:T(8,128)S(1)}, f32[16,16,256]{2,1,0:T(8,128)}, u32[]{:S(2)}) copy-start(f32[16,16,256]{2,1,0:T(8,128)} %refs_2_.1) | copy-start | bytes 786436

commit v3 on v2

--- a/solution.py
+++ b/solution.py
@@ -63,9 +63,8 @@
         *both("f2", H - 3),
         *both("f1", H - 3),
         *both("p0_d2", H - 3),
-        *faces("f0_d2", 2),
-        *both("f2_d2", 1),
-        *both("dp_d2", 1),
+        *faces("f0_d2", 1),
+        *both("dp2_x", 1),
     )
 
 
@@ -91,6 +90,7 @@
     "rhs": ("rhs2", 0, 7),
     "rhs_x": ("rhs2", 0, 7),
     "dp_x": ("dp", 0, 7),
+    "dp2_x": ("dp", 1, 6),
     "g2": ("rhs2", 1, 6),
     "g3": ("rhs3", 1, 6),
 }
@@ -584,7 +584,14 @@
 
     shared = {"t1": f1e, "tot": tote, "p0": p0e, "dp": dpe, "f0": f0e, "f2": f2e, "f1": f1e}
     shared |= {"p0_d2": p0e, "f0_d2": f0e, "f2_d2": f2e, "dp_d2": dpe, "rhs": rhse, "p1_d2": p1}
-    shared["dp_x"] = dpx
+    for e, beside, face in ((H - 1, H - 2, H - 2), (ext - H, ext - H + 1, ext - H)):
+        across = f2e[e]
+        p = p1[e]
+        beyond = f0e[face] * p1[beside] + across * roll(p, -1, 1) + roll(across * p, 1, 1)
+        g2u[e] = g2u[e] + beyond
+        g2d[e] = g2d[e] + beyond
+        dpx[e] = dpe[e] + f0e[face]
+    shared["dp_x"] = shared["dp2_x"] = dpx
     up = shared | {"g2": g2u, "g3": g3u, "rhs_x": rxu}
     down = shared | {"g2": g2d, "g3": g3d, "rhs_x": rxd}
     pack_both(x_near, x_cross, late_parts(layers), up, down, rows, gx)

time: 29.2 us -> 29 us (level)
  no operation moved by 1% of the time
where the time goes in v3:
time: 29 us; the launch traced here: 28.8 us
  starting transfers between devices  11.9 us (41%)
  Pallas kernels  9.86 us (34%)
  waiting for transfers between devices  6.22 us (21%)
  between operations  0.77 us (3%)
    pallas_call x6, Pallas kernels, call(): pl.pallas_call(kernel, out_shape=[as_struct(s) for s in outs], in_specs=[...  9.86 us
    ppermute x6, starting transfers between devices, swap(): return lax.ppermute(block, axis, pairs + [(b, a) for a, b in pairs])  8.51 us
    ppermute x6, waiting for transfers between devices, swap(): return lax.ppermute(block, axis, pairs + [(b, a) for a, b in pairs])  5.18 us
    ppermute x1, starting transfers between devices, body(): sums = sums + lax.ppermute(tile, 'gz', pairs)[:sums.shape[0]]  3.4 us
    ppermute x1, waiting for transfers between devices, body(): sums = sums + lax.ppermute(tile, 'gz', pairs)[:sums.shape[0]]  1.05 us
  transfers between devices with their start and end apart: 7, of which 3 were waited for; matrix products, arithmetic and copies ran while one was open for 0% of the time, Pallas kernels for 12%

profile of v3, /device:TPU:24, one launch (start us, length us, event | category | flops | bytes accessed | tf_op | source)
XLA Modules:
  0.0 28.8 jit_solution(11557002755925419471)
XLA Ops:
  0.6 2.4 %shard_map.137 = (f32[26,16,256]{2,1,0:T(8,128)S(1)}, f32[26,16,256]{2,1,0:T(8,128)S(1)}, f32[26,16,256]{2,1,0:T(8,128)S(1)}, f32[26,16,256]{2,1,0:T(8,128)S(1)}...) custom-call(f32[16,16,256]{2,1,0:T(8,128)} %refs_0_.1, ...), custom_call_target="tpu_custom_call" | custom-call | tf_op jit(solution)/shard_map/pallas_call | solution.py:680
  3.1 0.1 collective-permute-start.2
  3.1 0.7 %collective-permute-start = (f32[28,16,256]{2,1,0:T(8,128)S(1)}, f32[28,16,256]{2,1,0:T(8,128)S(1)}, u32[]{:S(2)}, u32[]{:S(2)}) collective-permute-start(f32[28,16,256]{2,1,0:T(8,128)S(1)} %get-tuple-element.83), channel_id=1, source_target_pairs={{1,2},{2,1},{5,6},{6,5},{9,10},{10,9},{13,14},{14,13},{17,18},{18,... | collective-permute-start | bytes 1376264 | tf_op jit(solution)/shard_map/ppermute | solution.py:666
  3.8 0.9 %shard_map.138 = (f32[26,16,256]{2,1,0:T(8,128)S(1)}, f32[26,16,256]{2,1,0:T(8,128)S(1)}, f32[26,16,256]{2,1,0:T(8,128)S(1)}, f32[26,16,256]{2,1,0:T(8,128)S(1)}...) custom-call(f32[26,16,256]{2,1,0:T(8,128)S(1)} %get-tuple-element.69, ...), custom_call_target="tpu_custom_call" | custom-call | tf_op jit(solution)/shard_map/pallas_call | solution.py:680
  4.7 1.6 %collective-permute-start.1 = (f32[24,8,256]{2,1,0:T(8,128)S(1)}, f32[24,8,256]{2,1,0:T(8,128)S(1)}, u32[]{:S(2)}, u32[]{:S(2)}) collective-permute-start(f32[24,8,256]{2,1,0:T(8,128)S(1)} %get-tuple-element.84), channel_id=1, source_target_pairs={{0,4},{8,12},{16,20},{24,28},{4,0},{12,8},{20,16},{28,24},{1,5},{9... | collective-permute-start | bytes 589832 | tf_op jit(solution)/shard_map/ppermute | solution.py:666
  6.3 0.0 collective-permute-done.2.refs_12_
  6.3 3.4 %collective-permute-start.3 = (f32[8,128]{1,0:T(8,128)S(1)}, f32[8,128]{1,0:T(8,128)S(1)}, u32[]{:S(2)}, u32[]{:S(2)}) collective-permute-start(f32[8,128]{1,0:T(8,128)S(1)} %pad.4), channel_id=1, source_target_pairs={{0,2},{1,3},{2,0},{3,1},{4,6},{5,7},{6,4},{7,5},{8,10},{9,11},{10,... | collective-permute-start | bytes 12296 | tf_op jit(solution)/shard_map/ppermute | solution.py:764
  9.7 2.3 %collective-permute-start.4 = (f32[24,8,256]{2,1,0:T(8,128)S(1)}, f32[24,8,256]{2,1,0:T(8,128)S(1)}, u32[]{:S(2)}, u32[]{:S(2)}) collective-permute-start(f32[24,8,256]{2,1,0:T(8,128)S(1)} %get-tuple-element.106), channel_id=1, source_target_pairs={{4,8},{12,16},{20,24},{8,4},{16,12},{24,20},{5,9},{13,17},{21,25},... | collective-permute-start | bytes 589832 | tf_op jit(solution)/shard_map/ppermute | solution.py:666
  12.0 0.0 collective-permute-done.1.near
  12.0 0.0 collective-permute-done.refs_11_
  12.0 0.6 %shard_map.139 = (f32[26,16,256]{2,1,0:T(8,128)S(1)}, f32[26,16,256]{2,1,0:T(8,128)S(1)}, f32[26,16,256]{2,1,0:T(8,128)S(1)}, f32[26,16,256]{2,1,0:T(8,128)S(1)}...) custom-call(f32[26,16,256]{2,1,0:T(8,128)S(1)} %get-tuple-element.69, ...), custom_call_target="tpu_custom_call", output_to_operand_aliasing={{0}: (0, {}), {1}: (1, {}), {2}: (2, {}), {3}: (3, {}), {4}... | custom-call | tf_op jit(solution)/shard_map/pallas_call | solution.py:680
  12.6 1.0 %collective-permute-done.3 = f32[8,128]{1,0:T(8,128)S(1)} collective-permute-done((f32[8,128]{1,0:T(8,128)S(1)}, f32[8,128]{1,0:T(8,128)S(1)}, u32[]{:S(2)}, u32[]{:S(2)}) %collective-permute-start.3) | collective-permute-done | bytes 4128 | tf_op jit(solution)/shard_map/ppermute | solution.py:764
  13.7 1.3 %shard_map.140 = (f32[26,16,256]{2,1,0:T(8,128)S(1)}, f32[16,16,256]{2,1,0:T(8,128)S(1)}, f32[16,8,256]{2,1,0:T(8,128)S(1)}, f32[16,8,256]{2,1,0:T(8,128)S(1)}, f32[1,128]{1,0:T(1,128)S(1)}) custom-call(f32[26,16,256]{2,1,0:T(8,128)S(1)} %get-tuple-element.90.refs_0_.refs_5_, f32[26,16,256]{2,1,0:T(8,128)S(1)} %get-tuple-element.91.refs_1_, ...), custom_call_target="tpu_custom_call" | custom-call | tf_op jit(solution)/shard_map/pallas_call | solution.py:680
  15.0 1.6 %collective-permute-start.5 = (f32[16,8,256]{2,1,0:T(8,128)S(1)}, f32[16,8,256]{2,1,0:T(8,128)S(1)}, u32[]{:S(2)}, u32[]{:S(2)}) collective-permute-start(f32[16,8,256]{2,1,0:T(8,128)S(1)} %get-tuple-element.109), channel_id=1, source_target_pairs={{0,4},{8,12},{16,20},{24,28},{4,0},{12,8},{20,16},{28,24},{1,5},{9... | collective-permute-start | bytes 393224 | tf_op jit(solution)/shard_map/ppermute | solution.py:666
  16.6 2.3 %collective-permute-start.6 = (f32[16,8,256]{2,1,0:T(8,128)S(1)}, f32[16,8,256]{2,1,0:T(8,128)S(1)}, u32[]{:S(2)}, u32[]{:S(2)}) collective-permute-start(f32[16,8,256]{2,1,0:T(8,128)S(1)} %get-tuple-element.110), channel_id=1, source_target_pairs={{4,8},{12,16},{20,24},{8,4},{16,12},{24,20},{5,9},{13,17},{21,25},... | collective-permute-start | bytes 393224 | tf_op jit(solution)/shard_map/ppermute | solution.py:666
  18.8 0.0 collective-permute-done.4.cross
  18.9 0.0 copy-start
  18.9 0.0 copy-start.1
  18.9 0.0 copy-start.2
  18.9 0.0 copy-start.3
  18.9 0.8 %shard_map.141 = (f32[26,8,256]{2,1,0:T(8,128)S(1)}, f32[26,8,256]{2,1,0:T(8,128)S(1)}, f32[26,8,256]{2,1,0:T(8,128)S(1)}, f32[26,8,256]{2,1,0:T(8,128)S(1)}, f3...) custom-call(f32[24,8,256]{2,1,0:T(8,128)S(1)} %collective-permute-do, ...), custom_call_target="tpu_custom_call" | custom-call | tf_op jit(solution)/shard_map/pallas_call | solution.py:680
  19.7 1.6 %collective-permute-done.5.refs_13_ = f32[16,8,256]{2,1,0:T(8,128)S(1)} collective-permute-done((f32[16,8,256]{2,1,0:T(8,128)S(1)}, f32[16,8,256]{2,1,0:T(8,128)S(1)}, u32[]{:S(2)}, u32[]{:S(2)}) %collective-permute-start.5) | collective-permute-done | bytes 131104 | tf_op jit(solution)/shard_map/ppermute | solution.py:666
  21.3 3.5 %collective-permute-done.6.refs_14_ = f32[16,8,256]{2,1,0:T(8,128)S(1)} collective-permute-done((f32[16,8,256]{2,1,0:T(8,128)S(1)}, f32[16,8,256]{2,1,0:T(8,128)S(1)}, u32[]{:S(2)}, u32[]{:S(2)}) %collective-permute-start.6) | collective-permute-done | bytes 131104 | tf_op jit(solution)/shard_map/ppermute | solution.py:666
  24.9 0.0 copy-done
  24.9 0.0 copy-done.1
  24.9 0.0 copy-done.2
  24.9 0.0 copy-done.3
  24.9 3.9 %shard_map.142 = (f32[16,16,256]{2,1,0:T(8,128)}, f32[16,16,256]{2,1,0:T(8,128)}, f32[16,16,256]{2,1,0:T(8,128)}, f32[16,16,256]{2,1,0:T(8,128)}, f32[1,32]{1,0:...) custom-call(f32[16,16,256]{2,1,0:T(8,128)S(1)} %copy-done, ...), custom_call_target="tpu_custom_call", output_to_operand_aliasing={{5}: (15, {}), {6}: (16, {}), {7}: (17, {}), {8}: (18, {}),... | custom-call | tf_op jit(solution)/shard_map/pallas_call | solution.py:680
  (3 shorter events, 0.0 us)
Async XLA Ops:
  3.1 3.2 %collective-permute-start.2 = (f32[29,16,256]{2,1,0:T(8,128)S(1)}, f32[29,16,256]{2,1,0:T(8,128)S(1)}, u32[]{:S(2)}, u32[]{:S(2)}) collective-permute-start(f32[29,16,256]{2,1,0:T(8,128)S(1)} %get-tuple-element.85), channel_id=1, source_target_pairs={{0,1},{2,3},{1,0},{3,2},{4,5},{6,7},{5,4},{7,6},{8,9},{10,11},{9,8... | collective-permute-start | bytes 1425416 | tf_op jit(solution)/shard_map/ppermute | solution.py:666
  3.1 8.9 %collective-permute-start = (f32[28,16,256]{2,1,0:T(8,128)S(1)}, f32[28,16,256]{2,1,0:T(8,128)S(1)}, u32[]{:S(2)}, u32[]{:S(2)}) collective-permute-start(f32[28,16,256]{2,1,0:T(8,128)S(1)} %get-tuple-element.83), channel_id=1, source_target_pairs={{1,2},{2,1},{5,6},{6,5},{9,10},{10,9},{13,14},{14,13},{17,18},{18,... | collective-permute-start | bytes 1376264 | tf_op jit(solution)/shard_map/ppermute | solution.py:666
  4.7 7.3 %collective-permute-start.1 = (f32[24,8,256]{2,1,0:T(8,128)S(1)}, f32[24,8,256]{2,1,0:T(8,128)S(1)}, u32[]{:S(2)}, u32[]{:S(2)}) collective-permute-start(f32[24,8,256]{2,1,0:T(8,128)S(1)} %get-tuple-element.84), channel_id=1, source_target_pairs={{0,4},{8,12},{16,20},{24,28},{4,0},{12,8},{20,16},{28,24},{1,5},{9... | collective-permute-start | bytes 589832 | tf_op jit(solution)/shard_map/ppermute | solution.py:666
  6.3 7.4 %collective-permute-start.3 = (f32[8,128]{1,0:T(8,128)S(1)}, f32[8,128]{1,0:T(8,128)S(1)}, u32[]{:S(2)}, u32[]{:S(2)}) collective-permute-start(f32[8,128]{1,0:T(8,128)S(1)} %pad.4), channel_id=1, source_target_pairs={{0,2},{1,3},{2,0},{3,1},{4,6},{5,7},{6,4},{7,5},{8,10},{9,11},{10,... | collective-permute-start | bytes 12296 | tf_op jit(solution)/shard_map/ppermute | solution.py:764
  9.7 9.1 %collective-permute-start.4 = (f32[24,8,256]{2,1,0:T(8,128)S(1)}, f32[24,8,256]{2,1,0:T(8,128)S(1)}, u32[]{:S(2)}, u32[]{:S(2)}) collective-permute-start(f32[24,8,256]{2,1,0:T(8,128)S(1)} %get-tuple-element.106), channel_id=1, source_target_pairs={{4,8},{12,16},{20,24},{8,4},{16,12},{24,20},{5,9},{13,17},{21,25},... | collective-permute-start | bytes 589832 | tf_op jit(solution)/shard_map/ppermute | solution.py:666
  15.0 6.4 %collective-permute-start.5 = (f32[16,8,256]{2,1,0:T(8,128)S(1)}, f32[16,8,256]{2,1,0:T(8,128)S(1)}, u32[]{:S(2)}, u32[]{:S(2)}) collective-permute-start(f32[16,8,256]{2,1,0:T(8,128)S(1)} %get-tuple-element.109), channel_id=1, source_target_pairs={{0,4},{8,12},{16,20},{24,28},{4,0},{12,8},{20,16},{28,24},{1,5},{9... | collective-permute-start | bytes 393224 | tf_op jit(solution)/shard_map/ppermute | solution.py:666
  16.6 8.3 %collective-permute-start.6 = (f32[16,8,256]{2,1,0:T(8,128)S(1)}, f32[16,8,256]{2,1,0:T(8,128)S(1)}, u32[]{:S(2)}, u32[]{:S(2)}) collective-permute-start(f32[16,8,256]{2,1,0:T(8,128)S(1)} %get-tuple-element.110), channel_id=1, source_target_pairs={{4,8},{12,16},{20,24},{8,4},{16,12},{24,20},{5,9},{13,17},{21,25},... | collective-permute-start | bytes 393224 | tf_op jit(solution)/shard_map/ppermute | solution.py:666
  18.9 6.0 %copy-start = (f32[16,16,256]{2,1,0:T(8,128)S(1)}, f32[16,16,256]{2,1,0:T(8,128)}, u32[]{:S(2)}) copy-start(f32[16,16,256]{2,1,0:T(8,128)} %refs_0_.1) | copy-start | bytes 786436
  18.9 6.0 %copy-start.1 = (f32[16,16,256]{2,1,0:T(8,128)S(1)}, f32[16,16,256]{2,1,0:T(8,128)}, u32[]{:S(2)}) copy-start(f32[16,16,256]{2,1,0:T(8,128)} %refs_1_.1) | copy-start | bytes 786436
  18.9 6.0 %copy-start.2 = (f32[16,16,256]{2,1,0:T(8,128)S(1)}, f32[16,16,256]{2,1,0:T(8,128)}, u32[]{:S(2)}) copy-start(f32[16,16,256]{2,1,0:T(8,128)} %refs_3_.1) | copy-start | bytes 786436
  18.9 6.0 %copy-start.3 = (f32[16,16,256]{2,1,0:T(8,128)S(1)}, f32[16,16,256]{2,1,0:T(8,128)}, u32[]{:S(2)}) copy-start(f32[16,16,256]{2,1,0:T(8,128)} %refs_2_.1) | copy-start | bytes 786436

commit v4 on v3

--- a/solution.py
+++ b/solution.py
@@ -163,7 +163,7 @@
 
 def loop(first, last, step, carry):
     count = last - first
-    unroll = -(-count // -(-count // 10))
+    unroll = -(-count // -(-count // 16))
     groups = count // unroll
 
     def group(g, carry):

time: 29 us -> 29 us (level)
  no operation moved by 1% of the time
where the time goes in v4:
time: 29 us; the launch traced here: 28.8 us
  starting transfers between devices  11.9 us (41%)
  Pallas kernels  9.67 us (33%)
  waiting for transfers between devices  6.45 us (22%)
  between operations  0.77 us (3%)
    pallas_call x6, Pallas kernels, call(): pl.pallas_call(kernel, out_shape=[as_struct(s) for s in outs], in_specs=[...  9.67 us
    ppermute x6, starting transfers between devices, swap(): return lax.ppermute(block, axis, pairs + [(b, a) for a, b in pairs])  8.51 us
    ppermute x6, waiting for transfers between devices, swap(): return lax.ppermute(block, axis, pairs + [(b, a) for a, b in pairs])  5.27 us
    ppermute x1, starting transfers between devices, body(): sums = sums + lax.ppermute(tile, 'gz', pairs)[:sums.shape[0]]  3.4 us
    ppermute x1, waiting for transfers between devices, body(): sums = sums + lax.ppermute(tile, 'gz', pairs)[:sums.shape[0]]  1.18 us
  transfers between devices with their start and end apart: 7, of which 3 were waited for; matrix products, arithmetic and copies ran while one was open for 0% of the time, Pallas kernels for 12%

profile of v4, /device:TPU:24, one launch (start us, length us, event | category | flops | bytes accessed | tf_op | source)
XLA Modules:
  0.0 28.8 jit_solution(8074470807263129713)
XLA Ops:
  0.6 2.4 %shard_map.137 = (f32[26,16,256]{2,1,0:T(8,128)S(1)}, f32[26,16,256]{2,1,0:T(8,128)S(1)}, f32[26,16,256]{2,1,0:T(8,128)S(1)}, f32[26,16,256]{2,1,0:T(8,128)S(1)}...) custom-call(f32[16,16,256]{2,1,0:T(8,128)} %refs_0_.1, ...), custom_call_target="tpu_custom_call" | custom-call | tf_op jit(solution)/shard_map/pallas_call | solution.py:680
  3.1 0.1 collective-permute-start.2
  3.1 0.7 %collective-permute-start = (f32[28,16,256]{2,1,0:T(8,128)S(1)}, f32[28,16,256]{2,1,0:T(8,128)S(1)}, u32[]{:S(2)}, u32[]{:S(2)}) collective-permute-start(f32[28,16,256]{2,1,0:T(8,128)S(1)} %get-tuple-element.83), channel_id=1, source_target_pairs={{1,2},{2,1},{5,6},{6,5},{9,10},{10,9},{13,14},{14,13},{17,18},{18,... | collective-permute-start | bytes 1376264 | tf_op jit(solution)/shard_map/ppermute | solution.py:666
  3.8 0.7 %shard_map.138 = (f32[26,16,256]{2,1,0:T(8,128)S(1)}, f32[26,16,256]{2,1,0:T(8,128)S(1)}, f32[26,16,256]{2,1,0:T(8,128)S(1)}, f32[26,16,256]{2,1,0:T(8,128)S(1)}...) custom-call(f32[26,16,256]{2,1,0:T(8,128)S(1)} %get-tuple-element.69, ...), custom_call_target="tpu_custom_call" | custom-call | tf_op jit(solution)/shard_map/pallas_call | solution.py:680
  4.6 1.6 %collective-permute-start.1 = (f32[24,8,256]{2,1,0:T(8,128)S(1)}, f32[24,8,256]{2,1,0:T(8,128)S(1)}, u32[]{:S(2)}, u32[]{:S(2)}) collective-permute-start(f32[24,8,256]{2,1,0:T(8,128)S(1)} %get-tuple-element.84), channel_id=1, source_target_pairs={{0,4},{8,12},{16,20},{24,28},{4,0},{12,8},{20,16},{28,24},{1,5},{9... | collective-permute-start | bytes 589832 | tf_op jit(solution)/shard_map/ppermute | solution.py:666
  6.2 0.0 collective-permute-done.2.refs_12_
  6.2 3.4 %collective-permute-start.3 = (f32[8,128]{1,0:T(8,128)S(1)}, f32[8,128]{1,0:T(8,128)S(1)}, u32[]{:S(2)}, u32[]{:S(2)}) collective-permute-start(f32[8,128]{1,0:T(8,128)S(1)} %pad.4), channel_id=1, source_target_pairs={{0,2},{1,3},{2,0},{3,1},{4,6},{5,7},{6,4},{7,5},{8,10},{9,11},{10,... | collective-permute-start | bytes 12296 | tf_op jit(solution)/shard_map/ppermute | solution.py:764
  9.6 2.3 %collective-permute-start.4 = (f32[24,8,256]{2,1,0:T(8,128)S(1)}, f32[24,8,256]{2,1,0:T(8,128)S(1)}, u32[]{:S(2)}, u32[]{:S(2)}) collective-permute-start(f32[24,8,256]{2,1,0:T(8,128)S(1)} %get-tuple-element.106), channel_id=1, source_target_pairs={{4,8},{12,16},{20,24},{8,4},{16,12},{24,20},{5,9},{13,17},{21,25},... | collective-permute-start | bytes 589832 | tf_op jit(solution)/shard_map/ppermute | solution.py:666
  11.9 0.0 collective-permute-done.1.near
  11.9 0.0 collective-permute-done.refs_11_
  11.9 0.6 %shard_map.139 = (f32[26,16,256]{2,1,0:T(8,128)S(1)}, f32[26,16,256]{2,1,0:T(8,128)S(1)}, f32[26,16,256]{2,1,0:T(8,128)S(1)}, f32[26,16,256]{2,1,0:T(8,128)S(1)}...) custom-call(f32[26,16,256]{2,1,0:T(8,128)S(1)} %get-tuple-element.69, ...), custom_call_target="tpu_custom_call", output_to_operand_aliasing={{0}: (0, {}), {1}: (1, {}), {2}: (2, {}), {3}: (3, {}), {4}... | custom-call | tf_op jit(solution)/shard_map/pallas_call | solution.py:680
  12.5 1.2 %collective-permute-done.3 = f32[8,128]{1,0:T(8,128)S(1)} collective-permute-done((f32[8,128]{1,0:T(8,128)S(1)}, f32[8,128]{1,0:T(8,128)S(1)}, u32[]{:S(2)}, u32[]{:S(2)}) %collective-permute-start.3) | collective-permute-done | bytes 4128 | tf_op jit(solution)/shard_map/ppermute | solution.py:764
  13.7 1.3 %shard_map.140 = (f32[26,16,256]{2,1,0:T(8,128)S(1)}, f32[16,16,256]{2,1,0:T(8,128)S(1)}, f32[16,8,256]{2,1,0:T(8,128)S(1)}, f32[16,8,256]{2,1,0:T(8,128)S(1)}, f32[1,128]{1,0:T(1,128)S(1)}) custom-call(f32[26,16,256]{2,1,0:T(8,128)S(1)} %get-tuple-element.90.refs_0_.refs_5_, f32[26,16,256]{2,1,0:T(8,128)S(1)} %get-tuple-element.91.refs_1_, ...), custom_call_target="tpu_custom_call" | custom-call | tf_op jit(solution)/shard_map/pallas_call | solution.py:680
  15.0 1.6 %collective-permute-start.5 = (f32[16,8,256]{2,1,0:T(8,128)S(1)}, f32[16,8,256]{2,1,0:T(8,128)S(1)}, u32[]{:S(2)}, u32[]{:S(2)}) collective-permute-start(f32[16,8,256]{2,1,0:T(8,128)S(1)} %get-tuple-element.109), channel_id=1, source_target_pairs={{0,4},{8,12},{16,20},{24,28},{4,0},{12,8},{20,16},{28,24},{1,5},{9... | collective-permute-start | bytes 393224 | tf_op jit(solution)/shard_map/ppermute | solution.py:666
  16.6 2.3 %collective-permute-start.6 = (f32[16,8,256]{2,1,0:T(8,128)S(1)}, f32[16,8,256]{2,1,0:T(8,128)S(1)}, u32[]{:S(2)}, u32[]{:S(2)}) collective-permute-start(f32[16,8,256]{2,1,0:T(8,128)S(1)} %get-tuple-element.110), channel_id=1, source_target_pairs={{4,8},{12,16},{20,24},{8,4},{16,12},{24,20},{5,9},{13,17},{21,25},... | collective-permute-start | bytes 393224 | tf_op jit(solution)/shard_map/ppermute | solution.py:666
  18.8 0.0 collective-permute-done.4.cross
  18.9 0.0 copy-start
  18.9 0.0 copy-start.1
  18.9 0.0 copy-start.2
  18.9 0.0 copy-start.3
  18.9 0.7 %shard_map.141 = (f32[26,8,256]{2,1,0:T(8,128)S(1)}, f32[26,8,256]{2,1,0:T(8,128)S(1)}, f32[26,8,256]{2,1,0:T(8,128)S(1)}, f32[26,8,256]{2,1,0:T(8,128)S(1)}, f3...) custom-call(f32[24,8,256]{2,1,0:T(8,128)S(1)} %collective-permute-do, ...), custom_call_target="tpu_custom_call" | custom-call | tf_op jit(solution)/shard_map/pallas_call | solution.py:680
  19.6 1.6 %collective-permute-done.5.refs_13_ = f32[16,8,256]{2,1,0:T(8,128)S(1)} collective-permute-done((f32[16,8,256]{2,1,0:T(8,128)S(1)}, f32[16,8,256]{2,1,0:T(8,128)S(1)}, u32[]{:S(2)}, u32[]{:S(2)}) %collective-permute-start.5) | collective-permute-done | bytes 131104 | tf_op jit(solution)/shard_map/ppermute | solution.py:666
  21.2 3.7 %collective-permute-done.6.refs_14_ = f32[16,8,256]{2,1,0:T(8,128)S(1)} collective-permute-done((f32[16,8,256]{2,1,0:T(8,128)S(1)}, f32[16,8,256]{2,1,0:T(8,128)S(1)}, u32[]{:S(2)}, u32[]{:S(2)}) %collective-permute-start.6) | collective-permute-done | bytes 131104 | tf_op jit(solution)/shard_map/ppermute | solution.py:666
  24.9 0.0 copy-done
  24.9 0.0 copy-done.1
  24.9 0.0 copy-done.2
  24.9 0.0 copy-done.3
  24.9 3.9 %shard_map.142 = (f32[16,16,256]{2,1,0:T(8,128)}, f32[16,16,256]{2,1,0:T(8,128)}, f32[16,16,256]{2,1,0:T(8,128)}, f32[16,16,256]{2,1,0:T(8,128)}, f32[1,32]{1,0:...) custom-call(f32[16,16,256]{2,1,0:T(8,128)S(1)} %copy-done, ...), custom_call_target="tpu_custom_call", output_to_operand_aliasing={{5}: (15, {}), {6}: (16, {}), {7}: (17, {}), {8}: (18, {}),... | custom-call | tf_op jit(solution)/shard_map/pallas_call | solution.py:680
  (3 shorter events, 0.0 us)
Async XLA Ops:
  3.1 3.1 %collective-permute-start.2 = (f32[29,16,256]{2,1,0:T(8,128)S(1)}, f32[29,16,256]{2,1,0:T(8,128)S(1)}, u32[]{:S(2)}, u32[]{:S(2)}) collective-permute-start(f32[29,16,256]{2,1,0:T(8,128)S(1)} %get-tuple-element.85), channel_id=1, source_target_pairs={{0,1},{2,3},{1,0},{3,2},{4,5},{6,7},{5,4},{7,6},{8,9},{10,11},{9,8... | collective-permute-start | bytes 1425416 | tf_op jit(solution)/shard_map/ppermute | solution.py:666
  3.1 8.7 %collective-permute-start = (f32[28,16,256]{2,1,0:T(8,128)S(1)}, f32[28,16,256]{2,1,0:T(8,128)S(1)}, u32[]{:S(2)}, u32[]{:S(2)}) collective-permute-start(f32[28,16,256]{2,1,0:T(8,128)S(1)} %get-tuple-element.83), channel_id=1, source_target_pairs={{1,2},{2,1},{5,6},{6,5},{9,10},{10,9},{13,14},{14,13},{17,18},{18,... | collective-permute-start | bytes 1376264 | tf_op jit(solution)/shard_map/ppermute | solution.py:666
  4.6 7.3 %collective-permute-start.1 = (f32[24,8,256]{2,1,0:T(8,128)S(1)}, f32[24,8,256]{2,1,0:T(8,128)S(1)}, u32[]{:S(2)}, u32[]{:S(2)}) collective-permute-start(f32[24,8,256]{2,1,0:T(8,128)S(1)} %get-tuple-element.84), channel_id=1, source_target_pairs={{0,4},{8,12},{16,20},{24,28},{4,0},{12,8},{20,16},{28,24},{1,5},{9... | collective-permute-start | bytes 589832 | tf_op jit(solution)/shard_map/ppermute | solution.py:666
  6.2 7.5 %collective-permute-start.3 = (f32[8,128]{1,0:T(8,128)S(1)}, f32[8,128]{1,0:T(8,128)S(1)}, u32[]{:S(2)}, u32[]{:S(2)}) collective-permute-start(f32[8,128]{1,0:T(8,128)S(1)} %pad.4), channel_id=1, source_target_pairs={{0,2},{1,3},{2,0},{3,1},{4,6},{5,7},{6,4},{7,5},{8,10},{9,11},{10,... | collective-permute-start | bytes 12296 | tf_op jit(solution)/shard_map/ppermute | solution.py:764
  9.6 9.3 %collective-permute-start.4 = (f32[24,8,256]{2,1,0:T(8,128)S(1)}, f32[24,8,256]{2,1,0:T(8,128)S(1)}, u32[]{:S(2)}, u32[]{:S(2)}) collective-permute-start(f32[24,8,256]{2,1,0:T(8,128)S(1)} %get-tuple-element.106), channel_id=1, source_target_pairs={{4,8},{12,16},{20,24},{8,4},{16,12},{24,20},{5,9},{13,17},{21,25},... | collective-permute-start | bytes 589832 | tf_op jit(solution)/shard_map/ppermute | solution.py:666
  15.0 6.2 %collective-permute-start.5 = (f32[16,8,256]{2,1,0:T(8,128)S(1)}, f32[16,8,256]{2,1,0:T(8,128)S(1)}, u32[]{:S(2)}, u32[]{:S(2)}) collective-permute-start(f32[16,8,256]{2,1,0:T(8,128)S(1)} %get-tuple-element.109), channel_id=1, source_target_pairs={{0,4},{8,12},{16,20},{24,28},{4,0},{12,8},{20,16},{28,24},{1,5},{9... | collective-permute-start | bytes 393224 | tf_op jit(solution)/shard_map/ppermute | solution.py:666
  16.6 8.3 %collective-permute-start.6 = (f32[16,8,256]{2,1,0:T(8,128)S(1)}, f32[16,8,256]{2,1,0:T(8,128)S(1)}, u32[]{:S(2)}, u32[]{:S(2)}) collective-permute-start(f32[16,8,256]{2,1,0:T(8,128)S(1)} %get-tuple-element.110), channel_id=1, source_target_pairs={{4,8},{12,16},{20,24},{8,4},{16,12},{24,20},{5,9},{13,17},{21,25},... | collective-permute-start | bytes 393224 | tf_op jit(solution)/shard_map/ppermute | solution.py:666
  18.9 6.0 %copy-start = (f32[16,16,256]{2,1,0:T(8,128)S(1)}, f32[16,16,256]{2,1,0:T(8,128)}, u32[]{:S(2)}) copy-start(f32[16,16,256]{2,1,0:T(8,128)} %refs_0_.1) | copy-start | bytes 786436
  18.9 6.0 %copy-start.1 = (f32[16,16,256]{2,1,0:T(8,128)S(1)}, f32[16,16,256]{2,1,0:T(8,128)}, u32[]{:S(2)}) copy-start(f32[16,16,256]{2,1,0:T(8,128)} %refs_1_.1) | copy-start | bytes 786436
  18.9 6.0 %copy-start.2 = (f32[16,16,256]{2,1,0:T(8,128)S(1)}, f32[16,16,256]{2,1,0:T(8,128)}, u32[]{:S(2)}) copy-start(f32[16,16,256]{2,1,0:T(8,128)} %refs_3_.1) | copy-start | bytes 786436
  18.9 6.0 %copy-start.3 = (f32[16,16,256]{2,1,0:T(8,128)S(1)}, f32[16,16,256]{2,1,0:T(8,128)}, u32[]{:S(2)}) copy-start(f32[16,16,256]{2,1,0:T(8,128)} %refs_2_.1) | copy-start | bytes 786436

commit v5 on v4

--- a/solution.py
+++ b/solution.py
@@ -131,6 +131,18 @@
             if place is not None:
                 seams[seam][e, place : place + 1, :] = message[at // 8, at % 8 : at % 8 + 1, :]
             at += 1
+
+
+def unpack_one(message, parts, seams, axis, first):
+    is_lower = lax.axis_index(axis) % 2 == first
+
+    @pl.when(is_lower)
+    def _():
+        unpack(message, parts, seams, 0)
+
+    @pl.when(jnp.logical_not(is_lower))
+    def _():
+        unpack(message, parts, seams, 1)
 
 
 def unpack_both(near, cross, parts, seams, gx):
@@ -597,18 +609,22 @@
     pack_both(x_near, x_cross, late_parts(layers), up, down, rows, gx)
 
 
+def near_kernel(near, *refs, layers, gx):
+    unpack_one(near, late_parts(layers), dict(zip(SEAMS, refs[len(SEAMS) :])), gx, 0)
+
+
 def finish_kernel(*refs, gx):
     sat, hist, volume, storage, source = refs[:5]
-    p0e, tote, frace, f0e, f1e, f2e, dpe, rhse, near, cross = refs[5:15]
-    hole = refs[19 + len(SEAMS)]
-    refs = refs[20 + len(SEAMS) :]
+    p0e, tote, frace, f0e, f1e, f2e, dpe, rhse, cross = refs[5:14]
+    hole = refs[18 + len(SEAMS)]
+    refs = refs[19 + len(SEAMS) :]
     new_p, residual, new_sat, new_hist, bottom = refs[:5]
     seams = dict(zip(SEAMS, refs[5:]))
     f1, rdiag, pa, pb = refs[5 + len(SEAMS) :]
     bottom[...] = hole[:, 0 : bottom.shape[1]]
     layers, rows, columns = sat.shape
     ext = layers + 2 * H
-    unpack_both(near, cross, late_parts(layers), seams, gx)
+    unpack_one(cross, late_parts(layers), seams, gx, 1)
     sfrac = seams["frac"]
     pa[0] = join(p0e[0], seams["p0"][0])
     pa[ext - 1] = join(p0e[ext - 1], seams["p0"][ext - 1])
@@ -825,6 +841,16 @@
         dpe,
         rhse,
     )
+    filled = list(filled)
+    count = len(SEAMS)
+    filled[:count] = call(
+        functools.partial(near_kernel, layers=layers, gx="gx"),
+        seams,
+        [],
+        late_near,
+        *filled[:count],
+        aliases={1 + i: i for i in range(count)},
+    )
     field, residual, new_sat, new_hist, bottom, *_ = call(
         functools.partial(finish_kernel, gx="gx"),
         [block] * 4 + [(1, wells)] + seams + joined,
@@ -842,11 +868,10 @@
         f2e,
         dpe,
         rhse,
-        late_near,
         late_cross,
         *filled,
         hole,
-        aliases={15 + i: 5 + i for i in range(len(filled))},
+        aliases={14 + i: 5 + i for i in range(len(filled))},
     )
     return (field, residual, new_sat, new_hist, bottom.reshape(wells))
 

time: 29 us -> 29.4 us (1.014)
  the two profiles are of different devices: /device:TPU:24 before, /device:TPU:10 now
where the time goes in v5:
time: 29.4 us; the launch traced here: 29.2 us
  starting transfers between devices  10.1 us (34%)
  Pallas kernels  9.55 us (32%)
  waiting for transfers between devices  7.74 us (26%)
  local copies, waits for them, and re-layouts  1.08 us (4%)
  between operations  0.75 us (3%)
    ppermute x6, starting transfers between devices, swap(): return lax.ppermute(block, axis, pairs + [(b, a) for a, b in pairs])  9.99 us
    pallas_call x7, Pallas kernels, call(): pl.pallas_call(kernel, out_shape=[as_struct(s) for s in outs], in_specs=[...  9.55 us
    ppermute x6, waiting for transfers between devices, swap(): return lax.ppermute(block, axis, pairs + [(b, a) for a, b in pairs])  7.74 us
    unnamed x8, local copies, waits for them, and re-layouts  1.07 us
  transfers between devices with their start and end apart: 7, of which 3 were waited for; matrix products, arithmetic and copies ran while one was open for 0% of the time, Pallas kernels for 12%

profile of v5, /device:TPU:10, one launch (start us, length us, event | category | flops | bytes accessed | tf_op | source)
XLA Modules:
  0.0 29.2 jit_solution(14584460987187891661)
XLA Ops:
  0.6 2.4 %shard_map.137 = (f32[26,16,256]{2,1,0:T(8,128)S(1)}, f32[26,16,256]{2,1,0:T(8,128)S(1)}, f32[26,16,256]{2,1,0:T(8,128)S(1)}, f32[26,16,256]{2,1,0:T(8,128)S(1)}...) custom-call(f32[16,16,256]{2,1,0:T(8,128)} %refs_0_.1, ...), custom_call_target="tpu_custom_call" | custom-call | tf_op jit(solution)/shard_map/pallas_call | solution.py:696
  3.1 0.1 collective-permute-start.2
  3.1 2.5 %collective-permute-start = (f32[28,16,256]{2,1,0:T(8,128)S(1)}, f32[28,16,256]{2,1,0:T(8,128)S(1)}, u32[]{:S(2)}, u32[]{:S(2)}) collective-permute-start(f32[28,16,256]{2,1,0:T(8,128)S(1)} %get-tuple-element.93), channel_id=1, source_target_pairs={{1,2},{2,1},{5,6},{6,5},{9,10},{10,9},{13,14},{14,13},{17,18},{18,... | collective-permute-start | bytes 1376264 | tf_op jit(solution)/shard_map/ppermute | solution.py:682
  5.7 0.7 %shard_map.138 = (f32[26,16,256]{2,1,0:T(8,128)S(1)}, f32[26,16,256]{2,1,0:T(8,128)S(1)}, f32[26,16,256]{2,1,0:T(8,128)S(1)}, f32[26,16,256]{2,1,0:T(8,128)S(1)}...) custom-call(f32[26,16,256]{2,1,0:T(8,128)S(1)} %get-tuple-element.79, ...), custom_call_target="tpu_custom_call" | custom-call | tf_op jit(solution)/shard_map/pallas_call | solution.py:696
  6.4 1.6 %collective-permute-start.1 = (f32[24,8,256]{2,1,0:T(8,128)S(1)}, f32[24,8,256]{2,1,0:T(8,128)S(1)}, u32[]{:S(2)}, u32[]{:S(2)}) collective-permute-start(f32[24,8,256]{2,1,0:T(8,128)S(1)} %get-tuple-element.94), channel_id=1, source_target_pairs={{0,4},{8,12},{16,20},{24,28},{4,0},{12,8},{20,16},{28,24},{1,5},{9... | collective-permute-start | bytes 589832 | tf_op jit(solution)/shard_map/ppermute | solution.py:682
  8.0 0.0 collective-permute-done.2.refs_12_
  8.0 0.1 collective-permute-start.3
  8.1 1.9 %collective-permute-start.4 = (f32[24,8,256]{2,1,0:T(8,128)S(1)}, f32[24,8,256]{2,1,0:T(8,128)S(1)}, u32[]{:S(2)}, u32[]{:S(2)}) collective-permute-start(f32[24,8,256]{2,1,0:T(8,128)S(1)} %get-tuple-element.116), channel_id=1, source_target_pairs={{4,8},{12,16},{20,24},{8,4},{16,12},{24,20},{5,9},{13,17},{21,25},... | collective-permute-start | bytes 589832 | tf_op jit(solution)/shard_map/ppermute | solution.py:682
  10.0 2.1 %collective-permute-done.1.near = f32[24,8,256]{2,1,0:T(8,128)S(1)} collective-permute-done((f32[24,8,256]{2,1,0:T(8,128)S(1)}, f32[24,8,256]{2,1,0:T(8,128)S(1)}, u32[]{:S(2)}, u32[]{:S(2)}) %collective-permute-start.1) | collective-permute-done | bytes 196640 | tf_op jit(solution)/shard_map/ppermute | solution.py:682
  12.2 0.8 %collective-permute-done.refs_11_ = f32[28,16,256]{2,1,0:T(8,128)S(1)} collective-permute-done((f32[28,16,256]{2,1,0:T(8,128)S(1)}, f32[28,16,256]{2,1,0:T(8,128)S(1)}, u32[]{:S(2)}, u32[]{:S(2)}) %collective-permute-start) | collective-permute-done | bytes 458784 | tf_op jit(solution)/shard_map/ppermute | solution.py:682
  13.0 0.6 %shard_map.139 = (f32[26,16,256]{2,1,0:T(8,128)S(1)}, f32[26,16,256]{2,1,0:T(8,128)S(1)}, f32[26,16,256]{2,1,0:T(8,128)S(1)}, f32[26,16,256]{2,1,0:T(8,128)S(1)}...) custom-call(f32[26,16,256]{2,1,0:T(8,128)S(1)} %get-tuple-element.79, ...), custom_call_target="tpu_custom_call", output_to_operand_aliasing={{0}: (0, {}), {1}: (1, {}), {2}: (2, {}), {3}: (3, {}), {4}... | custom-call | tf_op jit(solution)/shard_map/pallas_call | solution.py:696
  13.6 0.0 collective-permute-done.3
  13.6 1.2 %shard_map.140 = (f32[26,16,256]{2,1,0:T(8,128)S(1)}, f32[16,16,256]{2,1,0:T(8,128)S(1)}, f32[16,8,256]{2,1,0:T(8,128)S(1)}, f32[16,8,256]{2,1,0:T(8,128)S(1)}, f32[1,128]{1,0:T(1,128)S(1)}) custom-call(f32[26,16,256]{2,1,0:T(8,128)S(1)} %get-tuple-element.100.refs_0_.refs_5_, f32[26,16,256]{2,1,0:T(8,128)S(1)} %get-tuple-element.101.refs_1_, ...), custom_call_target="tpu_custom_call" | custom-call | tf_op jit(solution)/shard_map/pallas_call | solution.py:696
  14.9 1.6 %collective-permute-start.6 = (f32[16,8,256]{2,1,0:T(8,128)S(1)}, f32[16,8,256]{2,1,0:T(8,128)S(1)}, u32[]{:S(2)}, u32[]{:S(2)}) collective-permute-start(f32[16,8,256]{2,1,0:T(8,128)S(1)} %get-tuple-element.120), channel_id=1, source_target_pairs={{0,4},{8,12},{16,20},{24,28},{4,0},{12,8},{20,16},{28,24},{1,5},{9... | collective-permute-start | bytes 393224 | tf_op jit(solution)/shard_map/ppermute | solution.py:682
  16.4 2.3 %collective-permute-start.5 = (f32[16,8,256]{2,1,0:T(8,128)S(1)}, f32[16,8,256]{2,1,0:T(8,128)S(1)}, u32[]{:S(2)}, u32[]{:S(2)}) collective-permute-start(f32[16,8,256]{2,1,0:T(8,128)S(1)} %get-tuple-element.119), channel_id=1, source_target_pairs={{4,8},{12,16},{20,24},{8,4},{16,12},{24,20},{5,9},{13,17},{21,25},... | collective-permute-start | bytes 393224 | tf_op jit(solution)/shard_map/ppermute | solution.py:682
  18.7 0.0 collective-permute-done.4.cross
  18.8 0.7 %shard_map.141 = (f32[26,8,256]{2,1,0:T(8,128)S(1)}, f32[26,8,256]{2,1,0:T(8,128)S(1)}, f32[26,8,256]{2,1,0:T(8,128)S(1)}, f32[26,8,256]{2,1,0:T(8,128)S(1)}, f3...) custom-call(f32[24,8,256]{2,1,0:T(8,128)S(1)} %collective-permute-do, ...), custom_call_target="tpu_custom_call" | custom-call | tf_op jit(solution)/shard_map/pallas_call | solution.py:696
  19.5 4.8 %collective-permute-done.6.near = f32[16,8,256]{2,1,0:T(8,128)S(1)} collective-permute-done((f32[16,8,256]{2,1,0:T(8,128)S(1)}, f32[16,8,256]{2,1,0:T(8,128)S(1)}, u32[]{:S(2)}, u32[]{:S(2)}) %collective-permute-start.6) | collective-permute-done | bytes 131104 | tf_op jit(solution)/shard_map/ppermute | solution.py:682
  24.3 0.0 copy-start
  24.3 0.0 copy-start.1
  24.3 0.0 copy-start.2
  24.3 0.0 copy-start.3
  24.3 0.1 shard_map.142
  24.4 0.0 collective-permute-done.5.refs_13_
  24.4 0.8 %copy-done = f32[16,16,256]{2,1,0:T(8,128)S(1)} copy-done((f32[16,16,256]{2,1,0:T(8,128)S(1)}, f32[16,16,256]{2,1,0:T(8,128)}, u32[]{:S(2)}) %copy-start) | copy-done | bytes 262168
  25.2 0.1 copy-done.1
  25.3 0.1 copy-done.2
  25.4 0.1 copy-done.3
  25.4 3.8 %shard_map.143 = (f32[16,16,256]{2,1,0:T(8,128)}, f32[16,16,256]{2,1,0:T(8,128)}, f32[16,16,256]{2,1,0:T(8,128)}, f32[16,16,256]{2,1,0:T(8,128)}, f32[1,32]{1,0:...) custom-call(f32[16,16,256]{2,1,0:T(8,128)S(1)} %copy-done, ...), custom_call_target="tpu_custom_call", output_to_operand_aliasing={{5}: (14, {}), {6}: (15, {}), {7}: (16, {}), {8}: (17, {}),... | custom-call | tf_op jit(solution)/shard_map/pallas_call | solution.py:696
  (3 shorter events, 0.0 us)
Async XLA Ops:
  3.1 4.9 %collective-permute-start.2 = (f32[29,16,256]{2,1,0:T(8,128)S(1)}, f32[29,16,256]{2,1,0:T(8,128)S(1)}, u32[]{:S(2)}, u32[]{:S(2)}) collective-permute-start(f32[29,16,256]{2,1,0:T(8,128)S(1)} %get-tuple-element.95), channel_id=1, source_target_pairs={{0,1},{2,3},{1,0},{3,2},{4,5},{6,7},{5,4},{7,6},{8,9},{10,11},{9,8... | collective-permute-start | bytes 1425416 | tf_op jit(solution)/shard_map/ppermute | solution.py:682
  3.1 9.8 %collective-permute-start = (f32[28,16,256]{2,1,0:T(8,128)S(1)}, f32[28,16,256]{2,1,0:T(8,128)S(1)}, u32[]{:S(2)}, u32[]{:S(2)}) collective-permute-start(f32[28,16,256]{2,1,0:T(8,128)S(1)} %get-tuple-element.93), channel_id=1, source_target_pairs={{1,2},{2,1},{5,6},{6,5},{9,10},{10,9},{13,14},{14,13},{17,18},{18,... | collective-permute-start | bytes 1376264 | tf_op jit(solution)/shard_map/ppermute | solution.py:682
  6.4 5.7 %collective-permute-start.1 = (f32[24,8,256]{2,1,0:T(8,128)S(1)}, f32[24,8,256]{2,1,0:T(8,128)S(1)}, u32[]{:S(2)}, u32[]{:S(2)}) collective-permute-start(f32[24,8,256]{2,1,0:T(8,128)S(1)} %get-tuple-element.94), channel_id=1, source_target_pairs={{0,4},{8,12},{16,20},{24,28},{4,0},{12,8},{20,16},{28,24},{1,5},{9... | collective-permute-start | bytes 589832 | tf_op jit(solution)/shard_map/ppermute | solution.py:682
  8.0 5.6 %collective-permute-start.3 = (f32[8,128]{1,0:T(8,128)S(1)}, f32[8,128]{1,0:T(8,128)S(1)}, u32[]{:S(2)}, u32[]{:S(2)}) collective-permute-start(f32[8,128]{1,0:T(8,128)S(1)} %pad.4), channel_id=1, source_target_pairs={{0,2},{1,3},{2,0},{3,1},{4,6},{5,7},{6,4},{7,5},{8,10},{9,11},{10,... | collective-permute-start | bytes 12296 | tf_op jit(solution)/shard_map/ppermute | solution.py:780
  8.1 10.6 %collective-permute-start.4 = (f32[24,8,256]{2,1,0:T(8,128)S(1)}, f32[24,8,256]{2,1,0:T(8,128)S(1)}, u32[]{:S(2)}, u32[]{:S(2)}) collective-permute-start(f32[24,8,256]{2,1,0:T(8,128)S(1)} %get-tuple-element.116), channel_id=1, source_target_pairs={{4,8},{12,16},{20,24},{8,4},{16,12},{24,20},{5,9},{13,17},{21,25},... | collective-permute-start | bytes 589832 | tf_op jit(solution)/shard_map/ppermute | solution.py:682
  14.9 9.4 %collective-permute-start.6 = (f32[16,8,256]{2,1,0:T(8,128)S(1)}, f32[16,8,256]{2,1,0:T(8,128)S(1)}, u32[]{:S(2)}, u32[]{:S(2)}) collective-permute-start(f32[16,8,256]{2,1,0:T(8,128)S(1)} %get-tuple-element.120), channel_id=1, source_target_pairs={{0,4},{8,12},{16,20},{24,28},{4,0},{12,8},{20,16},{28,24},{1,5},{9... | collective-permute-start | bytes 393224 | tf_op jit(solution)/shard_map/ppermute | solution.py:682
  16.4 7.9 %collective-permute-start.5 = (f32[16,8,256]{2,1,0:T(8,128)S(1)}, f32[16,8,256]{2,1,0:T(8,128)S(1)}, u32[]{:S(2)}, u32[]{:S(2)}) collective-permute-start(f32[16,8,256]{2,1,0:T(8,128)S(1)} %get-tuple-element.119), channel_id=1, source_target_pairs={{4,8},{12,16},{20,24},{8,4},{16,12},{24,20},{5,9},{13,17},{21,25},... | collective-permute-start | bytes 393224 | tf_op jit(solution)/shard_map/ppermute | solution.py:682
  24.3 1.0 %copy-start = (f32[16,16,256]{2,1,0:T(8,128)S(1)}, f32[16,16,256]{2,1,0:T(8,128)}, u32[]{:S(2)}) copy-start(f32[16,16,256]{2,1,0:T(8,128)} %refs_0_.1) | copy-start | bytes 786436
  24.3 1.0 %copy-start.1 = (f32[16,16,256]{2,1,0:T(8,128)S(1)}, f32[16,16,256]{2,1,0:T(8,128)}, u32[]{:S(2)}) copy-start(f32[16,16,256]{2,1,0:T(8,128)} %refs_1_.1) | copy-start | bytes 786436
  24.3 1.1 %copy-start.2 = (f32[16,16,256]{2,1,0:T(8,128)S(1)}, f32[16,16,256]{2,1,0:T(8,128)}, u32[]{:S(2)}) copy-start(f32[16,16,256]{2,1,0:T(8,128)} %refs_3_.1) | copy-start | bytes 786436
  24.3 1.2 %copy-start.3 = (f32[16,16,256]{2,1,0:T(8,128)S(1)}, f32[16,16,256]{2,1,0:T(8,128)}, u32[]{:S(2)}) copy-start(f32[16,16,256]{2,1,0:T(8,128)} %refs_2_.1) | copy-start | bytes 786436

commit v6 on v4

--- a/solution.py
+++ b/solution.py
@@ -163,7 +163,7 @@
 
 def loop(first, last, step, carry):
     count = last - first
-    unroll = -(-count // -(-count // 16))
+    unroll = -(-count // -(-count // 26))
     groups = count // unroll
 
     def group(g, carry):

time: 29 us -> 28.6 us (0.986)
  Pallas kernels: 9.67 us -> 9.27 us
    pallas_call x6, Pallas kernels: 9.67 us -> 9.27 us  [call(): pl.pallas_call(kernel, out_shape=[as_struct(s) for s in outs], in_specs=[...]
  transfers between devices with their start and end apart: 7 -> 7, of which waited for: 3 -> 3; matrix products, arithmetic and copies ran while one was open for 0% -> 0% of each run, Pallas kernels for 12% -> 11%
where the time goes in v6:
time: 28.6 us; the launch traced here: 28.4 us
  starting transfers between devices  11.9 us (42%)
  Pallas kernels  9.27 us (32%)
  waiting for transfers between devices  6.44 us (23%)
  between operations  0.77 us (3%)
    pallas_call x6, Pallas kernels, call(): pl.pallas_call(kernel, out_shape=[as_struct(s) for s in outs], in_specs=[...  9.27 us
    ppermute x6, starting transfers between devices, swap(): return lax.ppermute(block, axis, pairs + [(b, a) for a, b in pairs])  8.51 us
    ppermute x6, waiting for transfers between devices, swap(): return lax.ppermute(block, axis, pairs + [(b, a) for a, b in pairs])  5.26 us
    ppermute x1, starting transfers between devices, body(): sums = sums + lax.ppermute(tile, 'gz', pairs)[:sums.shape[0]]  3.4 us
    ppermute x1, waiting for transfers between devices, body(): sums = sums + lax.ppermute(tile, 'gz', pairs)[:sums.shape[0]]  1.18 us
  transfers between devices with their start and end apart: 7, of which 3 were waited for; matrix products, arithmetic and copies ran while one was open for 0% of the time, Pallas kernels for 11%

profile of v6, /device:TPU:24, one launch (start us, length us, event | category | flops | bytes accessed | tf_op | source)
XLA Modules:
  0.0 28.4 jit_solution(6939690010861771657)
XLA Ops:
  0.6 2.4 %shard_map.137 = (f32[26,16,256]{2,1,0:T(8,128)S(1)}, f32[26,16,256]{2,1,0:T(8,128)S(1)}, f32[26,16,256]{2,1,0:T(8,128)S(1)}, f32[26,16,256]{2,1,0:T(8,128)S(1)}...) custom-call(f32[16,16,256]{2,1,0:T(8,128)} %refs_0_.1, ...), custom_call_target="tpu_custom_call" | custom-call | tf_op jit(solution)/shard_map/pallas_call | solution.py:680
  3.1 0.1 collective-permute-start.2
  3.1 0.7 %collective-permute-start = (f32[28,16,256]{2,1,0:T(8,128)S(1)}, f32[28,16,256]{2,1,0:T(8,128)S(1)}, u32[]{:S(2)}, u32[]{:S(2)}) collective-permute-start(f32[28,16,256]{2,1,0:T(8,128)S(1)} %get-tuple-element.83), channel_id=1, source_target_pairs={{1,2},{2,1},{5,6},{6,5},{9,10},{10,9},{13,14},{14,13},{17,18},{18,... | collective-permute-start | bytes 1376264 | tf_op jit(solution)/shard_map/ppermute | solution.py:666
  3.8 0.7 %shard_map.138 = (f32[26,16,256]{2,1,0:T(8,128)S(1)}, f32[26,16,256]{2,1,0:T(8,128)S(1)}, f32[26,16,256]{2,1,0:T(8,128)S(1)}, f32[26,16,256]{2,1,0:T(8,128)S(1)}...) custom-call(f32[26,16,256]{2,1,0:T(8,128)S(1)} %get-tuple-element.69, ...), custom_call_target="tpu_custom_call" | custom-call | tf_op jit(solution)/shard_map/pallas_call | solution.py:680
  4.6 1.6 %collective-permute-start.1 = (f32[24,8,256]{2,1,0:T(8,128)S(1)}, f32[24,8,256]{2,1,0:T(8,128)S(1)}, u32[]{:S(2)}, u32[]{:S(2)}) collective-permute-start(f32[24,8,256]{2,1,0:T(8,128)S(1)} %get-tuple-element.84), channel_id=1, source_target_pairs={{0,4},{8,12},{16,20},{24,28},{4,0},{12,8},{20,16},{28,24},{1,5},{9... | collective-permute-start | bytes 589832 | tf_op jit(solution)/shard_map/ppermute | solution.py:666
  6.2 0.0 collective-permute-done.2.refs_12_
  6.2 3.4 %collective-permute-start.3 = (f32[8,128]{1,0:T(8,128)S(1)}, f32[8,128]{1,0:T(8,128)S(1)}, u32[]{:S(2)}, u32[]{:S(2)}) collective-permute-start(f32[8,128]{1,0:T(8,128)S(1)} %pad.4), channel_id=1, source_target_pairs={{0,2},{1,3},{2,0},{3,1},{4,6},{5,7},{6,4},{7,5},{8,10},{9,11},{10,... | collective-permute-start | bytes 12296 | tf_op jit(solution)/shard_map/ppermute | solution.py:764
  9.6 2.3 %collective-permute-start.4 = (f32[24,8,256]{2,1,0:T(8,128)S(1)}, f32[24,8,256]{2,1,0:T(8,128)S(1)}, u32[]{:S(2)}, u32[]{:S(2)}) collective-permute-start(f32[24,8,256]{2,1,0:T(8,128)S(1)} %get-tuple-element.106), channel_id=1, source_target_pairs={{4,8},{12,16},{20,24},{8,4},{16,12},{24,20},{5,9},{13,17},{21,25},... | collective-permute-start | bytes 589832 | tf_op jit(solution)/shard_map/ppermute | solution.py:666
  11.9 0.0 collective-permute-done.1.near
  11.9 0.0 collective-permute-done.refs_11_
  11.9 0.6 %shard_map.139 = (f32[26,16,256]{2,1,0:T(8,128)S(1)}, f32[26,16,256]{2,1,0:T(8,128)S(1)}, f32[26,16,256]{2,1,0:T(8,128)S(1)}, f32[26,16,256]{2,1,0:T(8,128)S(1)}...) custom-call(f32[26,16,256]{2,1,0:T(8,128)S(1)} %get-tuple-element.69, ...), custom_call_target="tpu_custom_call", output_to_operand_aliasing={{0}: (0, {}), {1}: (1, {}), {2}: (2, {}), {3}: (3, {}), {4}... | custom-call | tf_op jit(solution)/shard_map/pallas_call | solution.py:680
  12.5 1.2 %collective-permute-done.3 = f32[8,128]{1,0:T(8,128)S(1)} collective-permute-done((f32[8,128]{1,0:T(8,128)S(1)}, f32[8,128]{1,0:T(8,128)S(1)}, u32[]{:S(2)}, u32[]{:S(2)}) %collective-permute-start.3) | collective-permute-done | bytes 4128 | tf_op jit(solution)/shard_map/ppermute | solution.py:764
  13.7 1.0 %shard_map.140 = (f32[26,16,256]{2,1,0:T(8,128)S(1)}, f32[16,16,256]{2,1,0:T(8,128)S(1)}, f32[16,8,256]{2,1,0:T(8,128)S(1)}, f32[16,8,256]{2,1,0:T(8,128)S(1)}, f32[1,128]{1,0:T(1,128)S(1)}) custom-call(f32[26,16,256]{2,1,0:T(8,128)S(1)} %get-tuple-element.90.refs_0_.refs_5_, f32[26,16,256]{2,1,0:T(8,128)S(1)} %get-tuple-element.91.refs_1_, ...), custom_call_target="tpu_custom_call" | custom-call | tf_op jit(solution)/shard_map/pallas_call | solution.py:680
  14.7 1.6 %collective-permute-start.5 = (f32[16,8,256]{2,1,0:T(8,128)S(1)}, f32[16,8,256]{2,1,0:T(8,128)S(1)}, u32[]{:S(2)}, u32[]{:S(2)}) collective-permute-start(f32[16,8,256]{2,1,0:T(8,128)S(1)} %get-tuple-element.109), channel_id=1, source_target_pairs={{0,4},{8,12},{16,20},{24,28},{4,0},{12,8},{20,16},{28,24},{1,5},{9... | collective-permute-start | bytes 393224 | tf_op jit(solution)/shard_map/ppermute | solution.py:666
  16.2 2.3 %collective-permute-start.6 = (f32[16,8,256]{2,1,0:T(8,128)S(1)}, f32[16,8,256]{2,1,0:T(8,128)S(1)}, u32[]{:S(2)}, u32[]{:S(2)}) collective-permute-start(f32[16,8,256]{2,1,0:T(8,128)S(1)} %get-tuple-element.110), channel_id=1, source_target_pairs={{4,8},{12,16},{20,24},{8,4},{16,12},{24,20},{5,9},{13,17},{21,25},... | collective-permute-start | bytes 393224 | tf_op jit(solution)/shard_map/ppermute | solution.py:666
  18.5 0.0 collective-permute-done.4.cross
  18.6 0.0 copy-start
  18.6 0.0 copy-start.1
  18.6 0.0 copy-start.2
  18.6 0.0 copy-start.3
  18.6 0.7 %shard_map.141 = (f32[26,8,256]{2,1,0:T(8,128)S(1)}, f32[26,8,256]{2,1,0:T(8,128)S(1)}, f32[26,8,256]{2,1,0:T(8,128)S(1)}, f32[26,8,256]{2,1,0:T(8,128)S(1)}, f3...) custom-call(f32[24,8,256]{2,1,0:T(8,128)S(1)} %collective-permute-do, ...), custom_call_target="tpu_custom_call" | custom-call | tf_op jit(solution)/shard_map/pallas_call | solution.py:680
  19.3 1.9 %collective-permute-done.5.refs_13_ = f32[16,8,256]{2,1,0:T(8,128)S(1)} collective-permute-done((f32[16,8,256]{2,1,0:T(8,128)S(1)}, f32[16,8,256]{2,1,0:T(8,128)S(1)}, u32[]{:S(2)}, u32[]{:S(2)}) %collective-permute-start.5) | collective-permute-done | bytes 131104 | tf_op jit(solution)/shard_map/ppermute | solution.py:666
  21.2 3.4 %collective-permute-done.6.refs_14_ = f32[16,8,256]{2,1,0:T(8,128)S(1)} collective-permute-done((f32[16,8,256]{2,1,0:T(8,128)S(1)}, f32[16,8,256]{2,1,0:T(8,128)S(1)}, u32[]{:S(2)}, u32[]{:S(2)}) %collective-permute-start.6) | collective-permute-done | bytes 131104 | tf_op jit(solution)/shard_map/ppermute | solution.py:666
  24.6 0.0 copy-done
  24.6 0.0 copy-done.1
  24.6 0.0 copy-done.2
  24.6 0.0 copy-done.3
  24.6 3.8 %shard_map.142 = (f32[16,16,256]{2,1,0:T(8,128)}, f32[16,16,256]{2,1,0:T(8,128)}, f32[16,16,256]{2,1,0:T(8,128)}, f32[16,16,256]{2,1,0:T(8,128)}, f32[1,32]{1,0:...) custom-call(f32[16,16,256]{2,1,0:T(8,128)S(1)} %copy-done, ...), custom_call_target="tpu_custom_call", output_to_operand_aliasing={{5}: (15, {}), {6}: (16, {}), {7}: (17, {}), {8}: (18, {}),... | custom-call | tf_op jit(solution)/shard_map/pallas_call | solution.py:680
  (3 shorter events, 0.0 us)
Async XLA Ops:
  3.1 3.1 %collective-permute-start.2 = (f32[29,16,256]{2,1,0:T(8,128)S(1)}, f32[29,16,256]{2,1,0:T(8,128)S(1)}, u32[]{:S(2)}, u32[]{:S(2)}) collective-permute-start(f32[29,16,256]{2,1,0:T(8,128)S(1)} %get-tuple-element.85), channel_id=1, source_target_pairs={{0,1},{2,3},{1,0},{3,2},{4,5},{6,7},{5,4},{7,6},{8,9},{10,11},{9,8... | collective-permute-start | bytes 1425416 | tf_op jit(solution)/shard_map/ppermute | solution.py:666
  3.1 8.7 %collective-permute-start = (f32[28,16,256]{2,1,0:T(8,128)S(1)}, f32[28,16,256]{2,1,0:T(8,128)S(1)}, u32[]{:S(2)}, u32[]{:S(2)}) collective-permute-start(f32[28,16,256]{2,1,0:T(8,128)S(1)} %get-tuple-element.83), channel_id=1, source_target_pairs={{1,2},{2,1},{5,6},{6,5},{9,10},{10,9},{13,14},{14,13},{17,18},{18,... | collective-permute-start | bytes 1376264 | tf_op jit(solution)/shard_map/ppermute | solution.py:666
  4.6 7.3 %collective-permute-start.1 = (f32[24,8,256]{2,1,0:T(8,128)S(1)}, f32[24,8,256]{2,1,0:T(8,128)S(1)}, u32[]{:S(2)}, u32[]{:S(2)}) collective-permute-start(f32[24,8,256]{2,1,0:T(8,128)S(1)} %get-tuple-element.84), channel_id=1, source_target_pairs={{0,4},{8,12},{16,20},{24,28},{4,0},{12,8},{20,16},{28,24},{1,5},{9... | collective-permute-start | bytes 589832 | tf_op jit(solution)/shard_map/ppermute | solution.py:666
  6.2 7.5 %collective-permute-start.3 = (f32[8,128]{1,0:T(8,128)S(1)}, f32[8,128]{1,0:T(8,128)S(1)}, u32[]{:S(2)}, u32[]{:S(2)}) collective-permute-start(f32[8,128]{1,0:T(8,128)S(1)} %pad.4), channel_id=1, source_target_pairs={{0,2},{1,3},{2,0},{3,1},{4,6},{5,7},{6,4},{7,5},{8,10},{9,11},{10,... | collective-permute-start | bytes 12296 | tf_op jit(solution)/shard_map/ppermute | solution.py:764
  9.6 9.0 %collective-permute-start.4 = (f32[24,8,256]{2,1,0:T(8,128)S(1)}, f32[24,8,256]{2,1,0:T(8,128)S(1)}, u32[]{:S(2)}, u32[]{:S(2)}) collective-permute-start(f32[24,8,256]{2,1,0:T(8,128)S(1)} %get-tuple-element.106), channel_id=1, source_target_pairs={{4,8},{12,16},{20,24},{8,4},{16,12},{24,20},{5,9},{13,17},{21,25},... | collective-permute-start | bytes 589832 | tf_op jit(solution)/shard_map/ppermute | solution.py:666
  14.7 6.6 %collective-permute-start.5 = (f32[16,8,256]{2,1,0:T(8,128)S(1)}, f32[16,8,256]{2,1,0:T(8,128)S(1)}, u32[]{:S(2)}, u32[]{:S(2)}) collective-permute-start(f32[16,8,256]{2,1,0:T(8,128)S(1)} %get-tuple-element.109), channel_id=1, source_target_pairs={{0,4},{8,12},{16,20},{24,28},{4,0},{12,8},{20,16},{28,24},{1,5},{9... | collective-permute-start | bytes 393224 | tf_op jit(solution)/shard_map/ppermute | solution.py:666
  16.2 8.3 %collective-permute-start.6 = (f32[16,8,256]{2,1,0:T(8,128)S(1)}, f32[16,8,256]{2,1,0:T(8,128)S(1)}, u32[]{:S(2)}, u32[]{:S(2)}) collective-permute-start(f32[16,8,256]{2,1,0:T(8,128)S(1)} %get-tuple-element.110), channel_id=1, source_target_pairs={{4,8},{12,16},{20,24},{8,4},{16,12},{24,20},{5,9},{13,17},{21,25},... | collective-permute-start | bytes 393224 | tf_op jit(solution)/shard_map/ppermute | solution.py:666
  18.6 6.0 %copy-start = (f32[16,16,256]{2,1,0:T(8,128)S(1)}, f32[16,16,256]{2,1,0:T(8,128)}, u32[]{:S(2)}) copy-start(f32[16,16,256]{2,1,0:T(8,128)} %refs_0_.1) | copy-start | bytes 786436
  18.6 6.0 %copy-start.1 = (f32[16,16,256]{2,1,0:T(8,128)S(1)}, f32[16,16,256]{2,1,0:T(8,128)}, u32[]{:S(2)}) copy-start(f32[16,16,256]{2,1,0:T(8,128)} %refs_1_.1) | copy-start | bytes 786436
  18.6 6.0 %copy-start.2 = (f32[16,16,256]{2,1,0:T(8,128)S(1)}, f32[16,16,256]{2,1,0:T(8,128)}, u32[]{:S(2)}) copy-start(f32[16,16,256]{2,1,0:T(8,128)} %refs_3_.1) | copy-start | bytes 786436
  18.6 6.0 %copy-start.3 = (f32[16,16,256]{2,1,0:T(8,128)S(1)}, f32[16,16,256]{2,1,0:T(8,128)}, u32[]{:S(2)}) copy-start(f32[16,16,256]{2,1,0:T(8,128)} %refs_2_.1) | copy-start | bytes 786436
